TPU v7x, 512 devices: a whole 4x4x16 slice. The times are simulated.
512 devices in a mesh: ctx: 64 (over y, z), uly: 8 (over x, core).
Axes of the slice: x: 4, y: 4, z: 16, core: 2. Of those that a mesh axis runs over, the one named last changes fastest.
Arguments:
- lin_query: bfloat16 [32768, 4096], P(('ctx', 'uly')), may hold values from -5 to 5
- lin_key: bfloat16 [32768, 4096], P(('ctx', 'uly')), may hold values from -5 to 5
- lin_value: bfloat16 [32768, 4096], P(('ctx', 'uly')), may hold values from -60 to 60
- log_decay: bfloat16 [32768, 32], P(('ctx', 'uly')), may hold values from 0 to 1
- norm_gain: float32 [4096], P('uly'), may hold values from 0.25 to 1.75
- doc_lengths: int32 [64], replicated, may hold values from 1 to 1024, 32768 in all
- att_query: bfloat16 [32768, 4096], P(('ctx', 'uly')), may hold values from -6 to 6
- att_key: bfloat16 [32768, 1024], P(('ctx', 'uly')), may hold values from -6 to 6
- att_value: bfloat16 [32768, 1024], P(('ctx', 'uly')), may hold values from -5 to 5
Outputs:
- lin_out: bfloat16 [32768, 4096], P('ctx', 'uly')
- att_out: bfloat16 [32768, 4096], P('ctx', 'uly')
Inputs may be any that keep to these rules, and one draw needn't show every extreme that they name: `doc_lengths`: documents follow one another from position 0 and fill the sequence; the longest has exactly 1024 positions.
All inputs are finite; a program needn't handle non-finite values.
Results may differ from a plain program's by a relative error of at most 0.008.
Values may be sent and summed in bfloat16 or wider, within the bound.
No kernel may reach another device: no remote copies, remote signals or barrier semaphores. Data moves between devices by JAX's collectives and lax.ppermute only.
A program may use at most 128 MiB of HBM per device.

v0:
```python
import jax
import jax.numpy as jnp
from jax import lax
from jax.sharding import PartitionSpec as P

HEAD = 128
WIN = 2


def prefix(x, axis, join, neutral):
    place = lax.axis_index(axis)
    gathered = jax.tree.map(
        lambda a, kind: lax.all_gather(a.astype(kind), axis), x, (jnp.bfloat16, jnp.bfloat16)
    )
    state = jax.tree.map(lambda a, e: jnp.zeros_like(a) + jnp.asarray(e, a.dtype), x, neutral)

    def one(turn, state):
        return join(
            state,
            jax.tree.map(
                lambda a, own: lax.dynamic_index_in_dim(a, turn, 0, False).astype(own.dtype),
                gathered,
                x,
            ),
        )

    return lax.fori_loop(0, place, one, state)


def shifted(block, axis, distance):
    devices = range(lax.axis_size(axis))
    route = [(i - distance, i) for i in devices if i - distance in devices]
    return lax.ppermute(block, axis, route)


def doc_begin(positions, doc_lengths):
    start_pos = jnp.cumsum(doc_lengths) - doc_lengths
    covered = start_pos[None, :] <= positions[:, None]
    return jnp.max(jnp.where(covered, start_pos[None, :], 0), axis=1)


def combine_states(earlier, later_part):
    return (earlier[0] * later_part[0], later_part[0][:, None, None] * earlier[1] + later_part[1])


def shards(
    lin_query, lin_key, lin_value, log_decay, norm_gain, doc_lengths, att_query, att_key, att_value
):
    query_in, key_in, value_in, decay_in, att_q, att_k, att_v = (
        lax.all_to_all(lin_query, "uly", split_axis=1, concat_axis=0, tiled=True),
        lax.all_to_all(lin_key, "uly", split_axis=1, concat_axis=0, tiled=True),
        lax.all_to_all(lin_value, "uly", split_axis=1, concat_axis=0, tiled=True),
        lax.all_to_all(log_decay, "uly", split_axis=1, concat_axis=0, tiled=True),
        lax.all_to_all(att_query, "uly", split_axis=1, concat_axis=0, tiled=True),
        lax.all_to_all(att_key, "uly", split_axis=1, concat_axis=0, tiled=True),
        lax.all_to_all(att_value, "uly", split_axis=1, concat_axis=0, tiled=True),
    )
    block_len = query_in.shape[0]
    head_count = decay_in.shape[1]
    block_start = lax.axis_index("ctx") * block_len
    offsets = jnp.arange(block_len, dtype=jnp.int32)
    positions = block_start + offsets
    token_begin = doc_begin(positions, doc_lengths)
    decay_sum = jnp.cumsum(decay_in.astype(jnp.float32), axis=0)
    query_map = jax.nn.silu(
        query_in.reshape(block_len, head_count, HEAD).astype(jnp.float32)
    ).astype(jnp.bfloat16)
    key_map = jax.nn.silu(key_in.reshape(block_len, head_count, HEAD).astype(jnp.float32)).astype(
        jnp.bfloat16
    )
    values = value_in.reshape(block_len, head_count, HEAD)
    scores = jnp.einsum("thd,shd->hts", query_map, key_map, preferred_element_type=jnp.float32)
    same_doc = (offsets[None, :] <= offsets[:, None]) & (
        token_begin[None, :] == token_begin[:, None]
    )
    decay_gap = decay_sum.T[:, :, None] - decay_sum.T[:, None, :]
    weights = jnp.where(same_doc[None], jnp.exp(-jnp.where(same_doc[None], decay_gap, 0.0)), 0.0)
    weighted_scores = (weights * scores).astype(jnp.bfloat16)
    inside = jnp.einsum("hts,shd->thd", weighted_scores, values, preferred_element_type=jnp.float32)
    last_begin = token_begin[block_len - 1]
    end_weight = jnp.where(
        (token_begin == last_begin)[:, None],
        jnp.exp(decay_sum - decay_sum[block_len - 1][None, :]),
        0.0,
    )
    end_keys = (key_map.astype(jnp.float32) * end_weight[:, :, None]).astype(jnp.bfloat16)
    end_state = jnp.einsum("shd,she->hde", end_keys, values, preferred_element_type=jnp.float32)
    block_decay = jnp.where(last_begin < block_start, jnp.exp(-decay_sum[block_len - 1]), 0.0)
    identity = (jnp.ones_like(block_decay), jnp.zeros_like(end_state))
    _, incoming = prefix((block_decay, end_state), "ctx", combine_states, identity)
    entry_decay = jnp.where((token_begin < block_start)[:, None], jnp.exp(-decay_sum), 0.0)
    carried = (
        jnp.einsum(
            "thd,hde->the",
            query_map,
            incoming.astype(jnp.bfloat16),
            preferred_element_type=jnp.float32,
        )
        * entry_decay[:, :, None]
    )
    combined = inside + carried
    normed = (
        combined
        * lax.rsqrt(jnp.mean(combined * combined, axis=-1, keepdims=True) + 1e-06)
        * norm_gain.reshape(head_count, HEAD)
    )
    lin_out = normed.astype(jnp.bfloat16).reshape(block_len, head_count * HEAD)
    kv_heads = att_k.shape[1] // HEAD
    group_size = att_q.shape[1] // (kv_heads * HEAD)
    queries = att_q.reshape(block_len, kv_heads, group_size, HEAD)
    score_scale = HEAD ** (-0.5)

    def attend(state_carry, key_block, value_block, key_position):
        row_max, row_total, accumulated = state_carry
        key_begin = doc_begin(key_position, doc_lengths)
        allowed = (
            (key_position[None, :] <= positions[:, None])
            & (key_position[None, :] >= 0)
            & (key_begin[None, :] == token_begin[:, None])
        )
        block_scores = (
            jnp.einsum(
                "tkgd,skd->kgts",
                queries,
                key_block.reshape(block_len, kv_heads, HEAD),
                preferred_element_type=jnp.float32,
            )
            * score_scale
        )
        new_max = jnp.maximum(row_max, jnp.max(jnp.where(allowed, block_scores, -1e30), axis=-1))
        att_weights = jnp.where(allowed, jnp.exp(block_scores - new_max[..., None]), 0.0)
        shrink = jnp.exp(row_max - new_max)
        row_total = row_total * shrink + jnp.sum(att_weights, axis=-1)
        products = jnp.einsum(
            "kgts,skd->tkgd",
            att_weights.astype(jnp.bfloat16),
            value_block.reshape(block_len, kv_heads, HEAD),
            preferred_element_type=jnp.float32,
        )
        accumulated = accumulated * jnp.transpose(shrink, (2, 0, 1))[..., None] + products
        return (new_max, row_total, accumulated)

    state_carry = (
        jnp.full((kv_heads, group_size, block_len), -1e30, jnp.float32),
        jnp.zeros((kv_heads, group_size, block_len), jnp.float32),
        jnp.zeros((block_len, kv_heads, group_size, HEAD), jnp.float32),
    )
    state_carry = attend(state_carry, att_k, att_v, positions)
    for distance in range(1, WIN + 1):
        earlier_keys, earlier_values = shifted((att_k, att_v), "ctx", distance)
        key_position = positions - distance * block_len
        state_carry = attend(state_carry, earlier_keys, earlier_values, key_position)
    row_max, row_total, accumulated = state_carry
    att_out = (
        (accumulated / jnp.transpose(row_total, (2, 0, 1))[..., None])
        .astype(jnp.bfloat16)
        .reshape(block_len, kv_heads * group_size * HEAD)
    )
    return (lin_out, att_out)


def solution(mesh):
    placed = (
        P(("ctx", "uly"), None),
        P(("ctx", "uly"), None),
        P(("ctx", "uly"), None),
        P(("ctx", "uly"), None),
        P("uly"),
        P(),
        P(("ctx", "uly"), None),
        P(("ctx", "uly"), None),
        P(("ctx", "uly"), None),
    )
    return jax.shard_map(
        shards,
        mesh=mesh,
        in_specs=placed,
        out_specs=(P("ctx", "uly"), P("ctx", "uly")),
        check_vma=False,
    )
```

profile of v0, /device:TPU:504, one launch (start us, length us, event | category | flops | bytes accessed | tf_op | source)
XLA Modules:
  0.0 326.5 jit_solution(10978063020451155656)
XLA Ops:
  8.6 4.3 %all-to-all-start = ((bf16[8,2,128]{2,1,0:T(2,128)(2,1)}), bf16[8,2,128]{2,1,0:T(2,128)(2,1)S(1)}, u32[]{:S(2)}, u32[]{:S(2)}) async-start(bf16[8,2,128]{2,1,0:T(2,128)(2,1)} %reshape.440), calls=%async_computation | async-start | bytes 8192 | tf_op jit(solution)/shard_map/all_to_all | solution.py:53
  17.2 1.9 copy.240
  19.1 1.9 copy.239
  20.9 4.8 %all-to-all-start.2 = ((bf16[64,8,512]{2,0,1:T(8,128)(2,1)}), bf16[64,8,512]{2,0,1:T(8,128)(2,1)S(1)}, u32[]{:S(2)}, u32[]{:S(2)}) async-start(bf16[64,8,512]{2,0,1:T(8,128)(2,1)} %bitcast.306), calls=%async_computation.2 | async-start | bytes 1048576 | tf_op jit(solution)/shard_map/all_to_all | solution.py:51
  28.3 7.8 %all-to-all-done.2 = bf16[64,8,512]{2,0,1:T(8,128)(2,1)S(1)} async-done(((bf16[64,8,512]{2,0,1:T(8,128)(2,1)}), bf16[64,8,512]{2,0,1:T(8,128)(2,1)S(1)}, u32[]{:S(2)}, u32[]{:S(2)}) %all-to-all-start.2) | async-done | bytes 524320 | tf_op jit(solution)/shard_map/all_to_all | solution.py:51
  36.1 3.5 %all-to-all-start.3 = ((bf16[64,8,512]{2,0,1:T(8,128)(2,1)}), bf16[64,8,512]{2,0,1:T(8,128)(2,1)S(1)}, u32[]{:S(2)}, u32[]{:S(2)}) async-start(bf16[64,8,512]{2,0,1:T(8,128)(2,1)} %bitcast.305), calls=%async_computation.3 | async-start | bytes 1048576 | tf_op jit(solution)/shard_map/all_to_all | solution.py:52
  41.2 8.7 %all-to-all-done.3 = bf16[64,8,512]{2,0,1:T(8,128)(2,1)S(1)} async-done(((bf16[64,8,512]{2,0,1:T(8,128)(2,1)}), bf16[64,8,512]{2,0,1:T(8,128)(2,1)S(1)}, u32[]{:S(2)}, u32[]{:S(2)}) %all-to-all-start.3) | async-done | bytes 524320 | tf_op jit(solution)/shard_map/all_to_all | solution.py:52
  52.2 4.0 %all-to-all-start.4 = ((bf16[64,8,128]{2,0,1:T(8,128)(2,1)}), bf16[64,8,128]{2,0,1:T(8,128)(2,1)}, u32[]{:S(2)}, u32[]{:S(2)}) async-start(bf16[64,8,128]{2,0,1:T(8,128)(2,1)} %copy_bitcast_fusion.5), calls=%async_computation.4 | async-start | bytes 262144 | tf_op jit(solution)/shard_map/all_to_all | solution.py:55
  56.9 5.4 %all-to-all-done.4 = bf16[64,8,128]{2,0,1:T(8,128)(2,1)} async-done(((bf16[64,8,128]{2,0,1:T(8,128)(2,1)}), bf16[64,8,128]{2,0,1:T(8,128)(2,1)}, u32[]{:S(2)}, u32[]{:S(2)}) %all-to-all-start.4) | async-done | bytes 131104 | tf_op jit(solution)/shard_map/all_to_all | solution.py:55
  62.3 3.4 %all-to-all-start.6 = ((bf16[64,8,128]{2,0,1:T(8,128)(2,1)}), bf16[64,8,128]{2,0,1:T(8,128)(2,1)S(1)}, u32[]{:S(2)}, u32[]{:S(2)}) async-start(bf16[64,8,128]{2,0,1:T(8,128)(2,1)} %copy_bitcast_fusion.4), calls=%async_computation.6 | async-start | bytes 262144 | tf_op jit(solution)/shard_map/all_to_all | solution.py:56
  66.6 5.2 %all-to-all-done.6 = bf16[64,8,128]{2,0,1:T(8,128)(2,1)S(1)} async-done(((bf16[64,8,128]{2,0,1:T(8,128)(2,1)}), bf16[64,8,128]{2,0,1:T(8,128)(2,1)S(1)}, u32[]{:S(2)}, u32[]{:S(2)}) %all-to-all-start.6) | async-done | bytes 131104 | tf_op jit(solution)/shard_map/all_to_all | solution.py:56
  71.8 3.5 %all-to-all-start.5 = ((bf16[64,8,512]{2,0,1:T(8,128)(2,1)}), bf16[64,8,512]{2,0,1:T(8,128)(2,1)S(1)}, u32[]{:S(2)}, u32[]{:S(2)}) async-start(bf16[64,8,512]{2,0,1:T(8,128)(2,1)} %bitcast.304), calls=%async_computation.5 | async-start | bytes 1048576 | tf_op jit(solution)/shard_map/all_to_all | solution.py:54
  75.3 2.4 compare_and_fusion
  79.8 70.3 %all-gather.1 = bf16[64,1,4]{2,1,0:T(2,128)(2,1)S(1)} all-gather(bf16[1,1,4]{2,1,0:T(2,128)(2,1)} %get-tuple-element.102), channel_id=1, replica_groups=mesh['ctx'=64,'uly'=8] {'ctx'}, dimensions={0}, use_global_device_ids=true | all-gather | bytes 520 | tf_op jit(solution)/shard_map/all_gather | solution.py:13
  158.0 5.2 %all-to-all-start.1 = ((bf16[64,8,512]{2,0,1:T(8,128)(2,1)}), bf16[64,8,512]{2,0,1:T(8,128)(2,1)S(1)}, u32[]{:S(2)}, u32[]{:S(2)}) async-start(bf16[64,8,512]{2,0,1:T(8,128)(2,1)} %bitcast.307), calls=%async_computation.1 | async-start | bytes 1048576 | tf_op jit(solution)/shard_map/all_to_all | solution.py:50
  163.3 1.8 fusion.6
  165.1 1.8 fusion
  167.0 1.8 fusion.3
  172.6 3.1 collective-permute-done.3
  175.7 2.0 fusion.29
  177.8 2.1 divide_convert_fusion
  181.4 3.5 %fusion.28 = f32[512,4,128]{0,2,1:T(8,128)S(1)} fusion(f32[4,512]{1,0:T(4,128)S(1)} %bitcast.327, pred[512,512]{1,0:T(8,128)(4,1)} %get-tuple-element.111, bf16[512,4,128]{2,1,0:T(4,128)(2,1)} %copy-done.4, f32[512,4,128]{2,1,0:T(4,128)S(1)} %reshape.426, f32[512,4,128]{2,1,0:T(4,128)S(1)} %reshape.427), kind=kOutput, calls=%fused_computation.34 | convolution fusion | flops 545783808 | bytes 3940352 | tf_op jit(solution)/shard_map/hts,shd->thd/dot_general | solution.py:79
  184.8 25.4 %all-gather.4.cloned.1.call-done = bf16[256,128,128]{2,1,0:T(8,128)(2,1)} async-done(((bf16[4,128,128]{2,1,0:T(8,128)(2,1)}), bf16[256,128,128]{2,1,0:T(8,128)(2,1)}) %all-gather.4.cloned.1.call-update) | async-done | bytes 8388624 | tf_op jit(solution)/shard_map/all_gather | solution.py:13
  210.3 107.6 %while.12 = (s32[]{:T(128)}, f32[4,128,128]{2,1,0:T(8,128)S(1)}, s32[]{:T(128)}, bf16[64,4]{1,0:T(8,128)(2,1)}, bf16[64,4,128,128]{3,2,1,0:T(8,128)(2,1)}, /*index=5*/s32[]{:T(128)}, s32[]{:T(128)}, s32[]{:T(128)}) while((s32[]{:T(128)}, f32[4,128,128]{2,1,0:T(8,128)S(1)}, s32[]{:T(128)}, bf16[64,4]{1,0:T(8,128)(2,1)}, ...), condition=%wide.region_5.6_spmd, body=%wide.region_4.5_spmd.sunk | while | flops 196617 | bytes 655527 | solution.py:27
  (216 shorter events, 135.8 us)
Async XLA Ops:
  7.2 44.3 %copy-start = (bf16[64,1024]{1,0:T(8,128)(2,1)S(1)}, bf16[64,1024]{1,0:T(8,128)(2,1)}, u32[]{:S(2)}) copy-start(bf16[64,1024]{1,0:T(8,128)(2,1)} %param.18) | copy-start | bytes 393220
  8.6 12.4 %all-to-all-start = ((bf16[8,2,128]{2,1,0:T(2,128)(2,1)}), bf16[8,2,128]{2,1,0:T(2,128)(2,1)S(1)}, u32[]{:S(2)}, u32[]{:S(2)}) async-start(bf16[8,2,128]{2,1,0:T(2,128)(2,1)} %reshape.440), calls=%async_computation | async-start | bytes 8192 | tf_op jit(solution)/shard_map/all_to_all | solution.py:53
  12.9 8.1 %copy-start.9 = (s32[512]{0:T(512)}, s32[512]{0:T(512)S(1)}, u32[]{:S(2)}) copy-start(s32[512]{0:T(512)S(1)} %get-tuple-element.123) | copy-start | bytes 6148
  12.9 8.0 %copy-start.8 = (s32[512]{0:T(512)}, s32[512]{0:T(512)S(1)}, u32[]{:S(2)}) copy-start(s32[512]{0:T(512)S(1)} %fusion.81) | copy-start | bytes 6148
  20.9 15.2 %all-to-all-start.2 = ((bf16[64,8,512]{2,0,1:T(8,128)(2,1)}), bf16[64,8,512]{2,0,1:T(8,128)(2,1)S(1)}, u32[]{:S(2)}, u32[]{:S(2)}) async-start(bf16[64,8,512]{2,0,1:T(8,128)(2,1)} %bitcast.306), calls=%async_computation.2 | async-start | bytes 1048576 | tf_op jit(solution)/shard_map/all_to_all | solution.py:51
  36.1 13.8 %all-to-all-start.3 = ((bf16[64,8,512]{2,0,1:T(8,128)(2,1)}), bf16[64,8,512]{2,0,1:T(8,128)(2,1)S(1)}, u32[]{:S(2)}, u32[]{:S(2)}) async-start(bf16[64,8,512]{2,0,1:T(8,128)(2,1)} %bitcast.305), calls=%async_computation.3 | async-start | bytes 1048576 | tf_op jit(solution)/shard_map/all_to_all | solution.py:52
  39.6 170.7 %all-gather.4.cloned.1.call-start = ((), (), s32[]{:S(2)}) async-start(), calls=%async_computation.7 | async-start | bytes 8519680 | tf_op jit(solution)/shard_map/all_gather | solution.py:13
  41.2 15.0 %copy-start.7 = (bf16[64,1024]{1,0:T(8,128)(2,1)S(1)}, bf16[64,1024]{1,0:T(8,128)(2,1)}, u32[]{:S(2)}) copy-start(bf16[64,1024]{1,0:T(8,128)(2,1)} %param.19) | copy-start | bytes 393220
  41.2 24.5 %copy-start.2 = (bf16[64,4096]{1,0:T(8,128)(2,1)S(1)}, bf16[64,4096]{1,0:T(8,128)(2,1)}, u32[]{:S(2)}) copy-start(bf16[64,4096]{1,0:T(8,128)(2,1)} %param.17) | copy-start | bytes 1572868
  50.0 21.8 %copy-start.4 = (bf16[512,4,128]{2,1,0:T(4,128)(2,1)}, bf16[512,4,128]{2,1,0:T(4,128)(2,1)S(1)}, u32[]{:S(2)}) copy-start(bf16[512,4,128]{2,1,0:T(4,128)(2,1)S(1)} %reshape.414) | copy-start | bytes 1572868
  51.5 27.5 %copy-start.3 = (bf16[64,4096]{1,0:T(8,128)(2,1)S(1)}, bf16[64,4096]{1,0:T(8,128)(2,1)}, u32[]{:S(2)}) copy-start(bf16[64,4096]{1,0:T(8,128)(2,1)} %param.11) | copy-start | bytes 1572868
  51.5 99.5 %copy-start.1 = (f32[512,4]{1,0:T(8,128)S(1)}, f32[512,4]{1,0:T(8,128)}, u32[]{:S(2)}) copy-start(f32[512,4]{1,0:T(8,128)} %get-tuple-element.100) | copy-start | bytes 24580
  52.2 10.1 %all-to-all-start.4 = ((bf16[64,8,128]{2,0,1:T(8,128)(2,1)}), bf16[64,8,128]{2,0,1:T(8,128)(2,1)}, u32[]{:S(2)}, u32[]{:S(2)}) async-start(bf16[64,8,128]{2,0,1:T(8,128)(2,1)} %copy_bitcast_fusion.5), calls=%async_computation.4 | async-start | bytes 262144 | tf_op jit(solution)/shard_map/all_to_all | solution.py:55
  62.3 9.4 %all-to-all-start.6 = ((bf16[64,8,128]{2,0,1:T(8,128)(2,1)}), bf16[64,8,128]{2,0,1:T(8,128)(2,1)S(1)}, u32[]{:S(2)}, u32[]{:S(2)}) async-start(bf16[64,8,128]{2,0,1:T(8,128)(2,1)} %copy_bitcast_fusion.4), calls=%async_computation.6 | async-start | bytes 262144 | tf_op jit(solution)/shard_map/all_to_all | solution.py:56
  71.8 3.5 %copy-start.5 = (bf16[64,8,128]{2,0,1:T(8,128)(2,1)}, bf16[64,8,128]{2,0,1:T(8,128)(2,1)S(1)}, u32[]{:S(2)}) copy-start(bf16[64,8,128]{2,0,1:T(8,128)(2,1)S(1)} %all-to-all-done.6) | copy-start | bytes 393220
  71.8 86.2 %all-to-all-start.5 = ((bf16[64,8,512]{2,0,1:T(8,128)(2,1)}), bf16[64,8,512]{2,0,1:T(8,128)(2,1)S(1)}, u32[]{:S(2)}, u32[]{:S(2)}) async-start(bf16[64,8,512]{2,0,1:T(8,128)(2,1)} %bitcast.304), calls=%async_computation.5 | async-start | bytes 1048576 | tf_op jit(solution)/shard_map/all_to_all | solution.py:54
  151.1 14.0 %collective-permute-start.2 = (bf16[512,128]{1,0:T(8,128)(2,1)}, bf16[512,128]{1,0:T(8,128)(2,1)}, u32[]{:S(2)}, u32[]{:S(2)}) collective-permute-start(bf16[512,128]{1,0:T(8,128)(2,1)} %bitcast.20), channel_id=1, source_target_pairs={{0,16},{8,24},{16,32},{24,40},{32,48},{40,56},{48,64},{56,72},{64,... | collective-permute-start | bytes 393224 | tf_op jit(solution)/shard_map/ppermute | solution.py:33
  152.4 14.6 %collective-permute-start = (bf16[512,128]{1,0:T(8,128)(2,1)}, bf16[512,128]{1,0:T(8,128)(2,1)}, u32[]{:S(2)}, u32[]{:S(2)}) collective-permute-start(bf16[512,128]{1,0:T(8,128)(2,1)} %bitcast.20), channel_id=1, source_target_pairs={{0,8},{8,16},{16,24},{24,32},{32,40},{40,48},{48,56},{56,64},{64,7... | collective-permute-start | bytes 393224 | tf_op jit(solution)/shard_map/ppermute | solution.py:33
  155.4 20.4 %collective-permute-start.3 = (bf16[512,128]{0,1:T(8,128)(2,1)}, bf16[512,128]{0,1:T(8,128)(2,1)}, u32[]{:S(2)}, u32[]{:S(2)}) collective-permute-start(bf16[512,128]{0,1:T(8,128)(2,1)} %copy.181), channel_id=1, source_target_pairs={{0,16},{8,24},{16,32},{24,40},{32,48},{40,56},{48,64},{56,72},{64,... | collective-permute-start | bytes 393224 | tf_op jit(solution)/shard_map/ppermute | solution.py:33
  156.6 21.1 %collective-permute-start.1 = (bf16[512,128]{0,1:T(8,128)(2,1)}, bf16[512,128]{0,1:T(8,128)(2,1)}, u32[]{:S(2)}, u32[]{:S(2)}) collective-permute-start(bf16[512,128]{0,1:T(8,128)(2,1)} %copy.181), channel_id=1, source_target_pairs={{0,8},{8,16},{16,24},{24,32},{32,40},{40,48},{48,56},{56,64},{64,7... | collective-permute-start | bytes 393224 | tf_op jit(solution)/shard_map/ppermute | solution.py:33
  158.0 22.9 %all-to-all-start.1 = ((bf16[64,8,512]{2,0,1:T(8,128)(2,1)}), bf16[64,8,512]{2,0,1:T(8,128)(2,1)S(1)}, u32[]{:S(2)}, u32[]{:S(2)}) async-start(bf16[64,8,512]{2,0,1:T(8,128)(2,1)} %bitcast.307), calls=%async_computation.1 | async-start | bytes 1048576 | tf_op jit(solution)/shard_map/all_to_all | solution.py:50
  169.7 1.9 copy-start.6
  210.3 108.2 %copy-start.10 = (f32[512]{0:T(512)S(1)}, f32[512]{0:T(512)}, u32[]{:S(2)}) copy-start(f32[512]{0:T(512)} %param.15) | copy-start | bytes 6148
Sparse Core Ops, SparseCore 0:
  51.6 158.5 all-gather.3
where the time goes:
time: 330 us; the launch traced here: 326 us
  other arithmetic  117 us (35%)
  blocking collectives  70.3 us (21%)
  waiting for transfers between devices  55.7 us (17%)
  starting transfers between devices  33.9 us (10%)
  local copies, waits for them, and re-layouts  17 us (5%)
  matrix products  16 us (5%)
  between operations  15.1 us (5%)
    all_gather x1, blocking collectives, prefix(): lax.all_gather(a.astype(kind), axis)  70.3 us
    add x63, other arithmetic, combine_states(): later_part[0][:, None, None] * earlier[1] + later_part[1]  63.7 us
    convert_element_type x63, other arithmetic, one(): lax.dynamic_index_in_dim(a, turn, 0, False).astype(own.dtype)  42.1 us
    all_gather x1, waiting for transfers between devices, prefix(): lax.all_gather(a.astype(kind), axis)  25.4 us
    all_to_all x1, waiting for transfers between devices, shards(): lax.all_to_all(lin_value, 'uly', split_axis=1, concat_axis=0, tiled=True)  8.67 us
    all_to_all x1, waiting for transfers between devices, shards(): lax.all_to_all(lin_key, 'uly', split_axis=1, concat_axis=0, tiled=True)  7.79 us
  transfers between devices with their start and end apart: 12, of which 6 were waited for; matrix products, arithmetic and copies ran while one was open for 12% of the time, Pallas kernels for 0%

commit v1 on v0

v1 whole, which is shorter than its diff:
```python
import functools

import jax
import jax.numpy as jnp
from jax import lax
from jax.experimental import pallas as pl
from jax.experimental.pallas import tpu as pltpu
from jax.sharding import PartitionSpec as P

HEAD = 128
PEERS = 8
TOK = 64
HEADS = 4
BLOCK = PEERS * TOK
REACH = 2 * BLOCK
ROW_TILE = 128
SPAN = REACH + ROW_TILE
DEC_ROW = 10 * TOK
ROWS_A = DEC_ROW + 16
ROWS_B = 12 * TOK
STATE_ROWS = HEADS * HEAD + 16
F32 = jnp.float32
BF16 = jnp.bfloat16
VMEM_LIMIT = 56 * 1024 * 1024


def silu(x):
    return x / (1.0 + jnp.exp(-x))


def call(body, out_shape, scratch=()):
    whole = pl.BlockSpec(memory_space=pltpu.VMEM)
    many = isinstance(out_shape, (tuple, list))
    return pl.pallas_call(
        body,
        out_shape=out_shape,
        out_specs=tuple(whole for _ in out_shape) if many else whole,
        scratch_shapes=list(scratch),
        compiler_params=pltpu.CompilerParams(vmem_limit_bytes=VMEM_LIMIT),
    )


def columns(out, source, first, count):
    for peer in range(PEERS):
        for i in range(count):
            column = (peer * count + i) * HEAD
            out[peer, (first + i) * TOK : (first + i + 1) * TOK, :] = source[:, column : column + HEAD]


def pack_first(k, v, ak, av, decay, out, window):
    columns(out, k, 0, HEADS)
    columns(out, v, 4, HEADS)
    columns(out, ak, 8, 1)
    columns(out, av, 9, 1)
    columns(window, ak, 0, 1)
    columns(window, av, 1, 1)
    turned = jnp.transpose(decay[...].astype(F32))
    turned = jnp.concatenate([turned, jnp.zeros((32, 64), F32)], axis=1)
    for peer in range(PEERS):
        rows = turned[HEADS * peer : HEADS * (peer + 1), :]
        rows = jnp.concatenate([rows, jnp.zeros((12, 128), F32)], axis=0)
        out[peer, DEC_ROW : DEC_ROW + 16, :] = rows.astype(BF16)


def pack_second(q, aq, kv1, kv2, out):
    columns(out, q, 0, HEADS)
    columns(out, aq, 4, HEADS)
    out[:, 8 * TOK : 10 * TOK, :] = kv1[...]
    out[:, 10 * TOK : 12 * TOK, :] = kv2[...]


def begins(lens):
    start = lax.axis_index("ctx") * BLOCK
    lane = lax.broadcasted_iota(jnp.int32, (8, 128), 1)
    row = jnp.concatenate([lens[...], jnp.zeros((1, 64), jnp.int32)], axis=1)
    row = jnp.broadcast_to(row, (8, 128))
    total = row
    for step in (1, 2, 4, 8, 16, 32):
        total = total + jnp.where(lane >= step, pltpu.roll(total, step, 1), 0)
    first = (total - row)[0:1, :] - start
    first = jnp.where(lane[0:1, :] < 64, first, 1 << 20)
    place = lax.broadcasted_iota(jnp.int32, (BLOCK, 128), 0)
    covered = jnp.where(first <= place, first, -(1 << 20))
    return jnp.max(covered.astype(F32), axis=1, keepdims=True).astype(jnp.int32)


def decay_rows(a):
    total = jnp.zeros((16, BLOCK), F32)
    for peer in range(PEERS):
        part = a[peer, DEC_ROW : DEC_ROW + 16, :]
        source = lax.broadcasted_iota(jnp.int32, (128, BLOCK), 0)
        place = lax.broadcasted_iota(jnp.int32, (128, BLOCK), 1)
        upto = jnp.where((source < TOK) & (source + peer * TOK <= place), 1.0, 0.0).astype(BF16)
        total = total + jnp.dot(part, upto, preferred_element_type=F32)
    return total


def gathered(a, index):
    return a[:, index * TOK : (index + 1) * TOK, :].reshape(BLOCK, HEAD)


def state(a, lens, out):
    begin = begins(lens)
    last = begin[BLOCK - 1 : BLOCK, :]
    rows = decay_rows(a)
    turned = jnp.transpose(rows)
    place = lax.broadcasted_iota(jnp.int32, (BLOCK, 1), 0)
    kept = place >= last
    extra = []
    for head in range(HEADS):
        sums = turned[:, head : head + 1]
        end = sums[BLOCK - 1 : BLOCK, :]
        weight = jnp.where(kept, jnp.exp(jnp.where(kept, sums - end, 0.0)), 0.0)
        key_map = silu(gathered(a, head).astype(F32)).astype(BF16).astype(F32)
        end_keys = (key_map * weight).astype(BF16)
        total = lax.dot_general(
            end_keys, gathered(a, 4 + head), (((0,), (0,)), ((), ())), preferred_element_type=F32
        )
        out[head * HEAD : (head + 1) * HEAD, :] = total.astype(BF16)
        extra.append(jnp.broadcast_to(jnp.where(last < 0, jnp.exp(-end), 0.0), (1, HEAD)))
    decay = jnp.concatenate([*extra, jnp.zeros((4, HEAD), F32)], axis=0)
    high = decay.astype(BF16).astype(F32)
    out[HEADS * HEAD :, :] = jnp.concatenate([high, decay - high], axis=0).astype(BF16)


def finish(a, b, near, far, lens, gain, lin_out, att_out, keys, values):
    begin = begins(lens)
    rows = decay_rows(a)
    turned = jnp.transpose(rows)
    shrink = near[HEADS * HEAD :, :].astype(F32)
    shrink = shrink[0:8, :] + shrink[8:16, :]
    for head in range(HEADS):
        query_map = silu(gathered(b, head).astype(F32)).astype(BF16)
        key_map = silu(gathered(a, head).astype(F32)).astype(BF16)
        value = gathered(a, 4 + head)
        piece = slice(head * HEAD, (head + 1) * HEAD)
        incoming = near[piece, :].astype(F32) + shrink[head : head + 1, :] * far[piece, :].astype(F32)
        carried = jnp.dot(query_map, incoming.astype(BF16), preferred_element_type=F32)
        sums = turned[:, head : head + 1]
        carried = carried * jnp.where(begin < 0, jnp.exp(-sums), 0.0)
        for tile in range(BLOCK // ROW_TILE):
            at = slice(tile * ROW_TILE, (tile + 1) * ROW_TILE)
            width = (tile + 1) * ROW_TILE
            scores = lax.dot_general(
                query_map[at], key_map[:width], (((1,), (1,)), ((), ())), preferred_element_type=F32
            )
            source = lax.broadcasted_iota(jnp.int32, (ROW_TILE, width), 1)
            place = lax.broadcasted_iota(jnp.int32, (ROW_TILE, width), 0) + tile * ROW_TILE
            allowed = (source <= place) & (source >= begin[at])
            gap = rows[head : head + 1, :width] - sums[at]
            weights = jnp.where(allowed, jnp.exp(jnp.where(allowed, gap, 0.0)), 0.0)
            inside = jnp.dot((weights * scores).astype(BF16), value[:width], preferred_element_type=F32)
            combined = inside + carried[at]
            mean = jnp.mean(combined * combined, axis=1, keepdims=True)
            normed = combined * lax.rsqrt(mean + 1e-6) * gain[:, piece]
            lin_out[at, piece] = normed.astype(BF16)

    for part, (ref, index) in enumerate(((b, 10), (b, 8), (a, 8))):
        keys[part * BLOCK : (part + 1) * BLOCK, :] = gathered(ref, index)
        values[part * BLOCK : (part + 1) * BLOCK, :] = gathered(ref, index + 1)
    for tile in range(BLOCK // ROW_TILE):
        at = slice(tile * ROW_TILE, (tile + 1) * ROW_TILE)
        near_keys = keys[tile * ROW_TILE : tile * ROW_TILE + SPAN, :]
        near_values = values[tile * ROW_TILE : tile * ROW_TILE + SPAN, :]
        source = lax.broadcasted_iota(jnp.int32, (ROW_TILE, SPAN), 1) - REACH
        place = lax.broadcasted_iota(jnp.int32, (ROW_TILE, SPAN), 0)
        allowed = (source <= place) & (source >= begin[at] - tile * ROW_TILE)
        for head in range(HEADS):
            query = b[2 * tile : 2 * tile + 2, (4 + head) * TOK : (5 + head) * TOK, :].reshape(ROW_TILE, HEAD)
            scores = lax.dot_general(
                query, near_keys, (((1,), (1,)), ((), ())), preferred_element_type=F32
            ) * (HEAD ** -0.5)
            scores = jnp.where(allowed, scores, -1e30)
            weights = jnp.exp(scores - jnp.max(scores, axis=1, keepdims=True))
            total = jnp.sum(weights, axis=1, keepdims=True)
            mixed = jnp.dot(weights.astype(BF16), near_values, preferred_element_type=F32)
            att_out[at, head * HEAD : (head + 1) * HEAD] = (mixed / total).astype(BF16)


def shifted(block, distance):
    count = lax.axis_size("ctx")
    return lax.ppermute(block, "ctx", [(i, i + distance) for i in range(count - distance)])


def exchanged(packed):
    return lax.all_to_all(packed, "uly", split_axis=0, concat_axis=0, tiled=True)


def shards(q, k, v, decay, gain, lens, aq, ak, av):
    lens = lens.reshape(1, 64)
    shape = lambda *dims: jax.ShapeDtypeStruct(dims, BF16)
    first, window = call(pack_first, (shape(PEERS, ROWS_A, HEAD), shape(PEERS, 2 * TOK, HEAD)))(k, v, ak, av, decay)
    a = exchanged(first)
    kv1, kv2 = shifted(window, 1), shifted(window, 2)
    second = call(pack_second, shape(PEERS, ROWS_B, HEAD))(q, aq, kv1, kv2)
    b = exchanged(second)
    own = call(state, shape(STATE_ROWS, HEAD))(a, lens)
    near, far = shifted(own, 1), shifted(own, 2)
    return call(
        finish,
        (shape(BLOCK, HEADS * HEAD), shape(BLOCK, HEADS * HEAD)),
        [pltpu.VMEM((3 * BLOCK, HEAD), BF16), pltpu.VMEM((3 * BLOCK, HEAD), BF16)],
    )(a, b, near, far, lens, gain.reshape(1, HEADS * HEAD))


def solution(mesh):
    rows = P(("ctx", "uly"), None)
    return jax.shard_map(
        shards,
        mesh=mesh,
        in_specs=(rows, rows, rows, rows, P("uly"), P(), rows, rows, rows),
        out_specs=(P("ctx", "uly"), P("ctx", "uly")),
        check_vma=False,
    )
```

time: 330 us -> 83 us (0.25)
  the two profiles are of different devices: /device:TPU:504 before, /device:TPU:56 now
where the time goes in v1:
time: 83 us; the launch traced here: 82.5 us
  waiting for transfers between devices  33.5 us (40%)
  starting transfers between devices  22.9 us (28%)
  Pallas kernels  21.1 us (25%)
  local copies, waits for them, and re-layouts  4.34 us (5%)
    ppermute x4, waiting for transfers between devices, shifted(): lax.ppermute(block, 'ctx', [(i, i + distance) for i in range(count - dist...  29.6 us
    ppermute x4, starting transfers between devices, shifted(): lax.ppermute(block, 'ctx', [(i, i + distance) for i in range(count - dist...  14 us
    pallas_call x1, Pallas kernels, shards(): call(finish, (shape(BLOCK, HEADS * HEAD), shape(BLOCK, HEADS * HEAD)), [p...  12.4 us
    all_to_all x2, starting transfers between devices, exchanged(): lax.all_to_all(packed, 'uly', split_axis=0, concat_axis=0, tiled=True)  8.88 us
    unnamed x15, local copies, waits for them, and re-layouts  4.34 us
    all_to_all x2, waiting for transfers between devices, exchanged(): lax.all_to_all(packed, 'uly', split_axis=0, concat_axis=0, tiled=True)  3.91 us
    pallas_call x1, Pallas kernels, shards(): own = call(state, shape(STATE_ROWS, HEAD))(a, lens)  3.31 us
    pallas_call x1, Pallas kernels, shards(): second = call(pack_second, shape(PEERS, ROWS_B, HEAD))(q, aq, kv1, kv2)  2.72 us
  transfers between devices with their start and end apart: 6, of which 5 were waited for; matrix products, arithmetic and copies ran while one was open for 0% of the time, Pallas kernels for 7%

profile of v1, /device:TPU:56, one launch (start us, length us, event | category | flops | bytes accessed | tf_op | source)
XLA Modules:
  0.0 82.5 jit_solution(4455317662913604767)
XLA Ops:
  0.6 1.4 %copy.11.decay = bf16[64,32]{1,0:T(8,128)(2,1)} copy(bf16[64,32]{0,1:T(8,128)(2,1)} %param.12) | data formatting | bytes 8192 | tf_op args[3]
  2.0 2.7 %shard_map.104 = (bf16[8,656,128]{2,1,0:T(8,128)(2,1)}, bf16[8,128,128]{2,1,0:T(8,128)(2,1)}) custom-call(bf16[64,4096]{1,0:T(8,128)(2,1)} %k.1, bf16[64,4096]{1,0:T(8,128)(2,1)} %v.1, bf16[64,1024]{1,0:T(8,128)(2,1)} %ak.1, bf16[64,1024]{1,0:T(8,128)(2,1)} %av.1, bf16[64,32]{1,0:T(8,128)(2,1)} %copy.11.decay), custom_call_target="tpu_custom_call" | custom-call | tf_op jit(solution)/shard_map/pallas_call | solution.py:192
  4.7 4.4 %all-to-all-start = ((bf16[8,656,128]{2,1,0:T(8,128)(2,1)}), bf16[8,656,128]{2,1,0:T(8,128)(2,1)S(1)}, u32[]{:S(2)}, u32[]{:S(2)}) async-start(bf16[8,656,128]{2,1,0:T(8,128)(2,1)} %get-tuple-element.4), calls=%async_computation | async-start | bytes 2686976 | tf_op jit(solution)/shard_map/all_to_all | solution.py:186
  9.1 0.0 copy-done.6
  9.1 3.8 %collective-permute-start = (bf16[8,128,128]{2,1,0:T(8,128)(2,1)S(1)}, bf16[8,128,128]{2,1,0:T(8,128)(2,1)S(1)}, u32[]{:S(2)}, u32[]{:S(2)}) collective-permute-start(bf16[8,128,128]{2,1,0:T(8,128)(2,1)S(1)} %copy-done.6), channel_id=1, source_target_pairs={{0,8},{8,16},{16,24},{24,32},{32,40},{40,48},{48,56},{56,64},{64,7... | collective-permute-start | bytes 786440 | tf_op jit(solution)/shard_map/ppermute | solution.py:182
  13.0 6.4 %collective-permute-start.1 = (bf16[8,128,128]{2,1,0:T(8,128)(2,1)S(1)}, bf16[8,128,128]{2,1,0:T(8,128)(2,1)S(1)}, u32[]{:S(2)}, u32[]{:S(2)}) collective-permute-start(bf16[8,128,128]{2,1,0:T(8,128)(2,1)S(1)} %copy-done.6), channel_id=1, source_target_pairs={{0,16},{8,24},{16,32},{24,40},{32,48},{40,56},{48,64},{56,72},{64,... | collective-permute-start | bytes 786440 | tf_op jit(solution)/shard_map/ppermute | solution.py:182
  19.4 5.6 %collective-permute-done.kv1 = bf16[8,128,128]{2,1,0:T(8,128)(2,1)S(1)} collective-permute-done((bf16[8,128,128]{2,1,0:T(8,128)(2,1)S(1)}, bf16[8,128,128]{2,1,0:T(8,128)(2,1)S(1)}, u32[]{:S(2)}, u32[]{:S(2)}) %collective-permute-start) | collective-permute-done | bytes 262176 | tf_op jit(solution)/shard_map/ppermute | solution.py:182
  24.9 13.5 %collective-permute-done.1.kv2 = bf16[8,128,128]{2,1,0:T(8,128)(2,1)S(1)} collective-permute-done((bf16[8,128,128]{2,1,0:T(8,128)(2,1)S(1)}, bf16[8,128,128]{2,1,0:T(8,128)(2,1)S(1)}, u32[]{:S(2)}, u32[]{:S(2)}) %collective-permute-start.1) | collective-permute-done | bytes 262176 | tf_op jit(solution)/shard_map/ppermute | solution.py:182
  38.5 0.0 copy-done.2
  38.5 0.7 copy-done.3
  39.2 2.7 %shard_map.105 = bf16[8,768,128]{2,1,0:T(8,128)(2,1)} custom-call(bf16[64,4096]{1,0:T(8,128)(2,1)} %q.1, bf16[64,4096]{1,0:T(8,128)(2,1)} %aq.1, bf16[8,128,128]{2,1,0:T(8,128)(2,1)} %copy-done.2, bf16[8,128,128]{2,1,0:T(8,128)(2,1)} %copy-done.3), custom_call_target="tpu_custom_call" | custom-call | tf_op jit(solution)/shard_map/pallas_call | solution.py:195
  41.9 0.0 all-to-all-done.a
  41.9 1.1 %copy-done = bf16[8,656,128]{2,1,0:T(8,128)(2,1)} copy-done((bf16[8,656,128]{2,1,0:T(8,128)(2,1)}, bf16[8,656,128]{2,1,0:T(8,128)(2,1)S(1)}, u32[]{:S(2)}) %copy-start) | copy-done | bytes 1343512
  43.0 4.4 %all-to-all-start.1 = ((bf16[8,768,128]{2,1,0:T(8,128)(2,1)}), bf16[8,768,128]{2,1,0:T(8,128)(2,1)S(1)}, u32[]{:S(2)}, u32[]{:S(2)}) async-start(bf16[8,768,128]{2,1,0:T(8,128)(2,1)} %shard_map.105), calls=%async_computation.1 | async-start | bytes 3145728 | tf_op jit(solution)/shard_map/all_to_all | solution.py:186
  47.4 3.3 %shard_map.106 = bf16[528,128]{1,0:T(8,128)(2,1)} custom-call(bf16[8,656,128]{2,1,0:T(8,128)(2,1)} %copy-done, s32[1,64]{1,0:T(1,128)} %bitcast.3), custom_call_target="tpu_custom_call" | custom-call | tf_op jit(solution)/shard_map/pallas_call | solution.py:197
  50.7 1.9 %collective-permute-start.2 = (bf16[528,128]{1,0:T(8,128)(2,1)}, bf16[528,128]{1,0:T(8,128)(2,1)S(1)}, u32[]{:S(2)}, u32[]{:S(2)}) collective-permute-start(bf16[528,128]{1,0:T(8,128)(2,1)} %shard_map.106), channel_id=1, source_target_pairs={{0,8},{8,16},{16,24},{24,32},{32,40},{40,48},{48,56},{56,64},{64,7... | collective-permute-start | bytes 405512 | tf_op jit(solution)/shard_map/ppermute | solution.py:182
  52.6 1.9 %collective-permute-start.3 = (bf16[528,128]{1,0:T(8,128)(2,1)}, bf16[528,128]{1,0:T(8,128)(2,1)S(1)}, u32[]{:S(2)}, u32[]{:S(2)}) collective-permute-start(bf16[528,128]{1,0:T(8,128)(2,1)} %shard_map.106), channel_id=1, source_target_pairs={{0,16},{8,24},{16,32},{24,40},{32,48},{40,56},{48,64},{56,72},{64,... | collective-permute-start | bytes 405512 | tf_op jit(solution)/shard_map/ppermute | solution.py:182
  54.6 4.6 %collective-permute-done.2.near = bf16[528,128]{1,0:T(8,128)(2,1)S(1)} collective-permute-done((bf16[528,128]{1,0:T(8,128)(2,1)}, bf16[528,128]{1,0:T(8,128)(2,1)S(1)}, u32[]{:S(2)}, u32[]{:S(2)}) %collective-permute-start.2) | collective-permute-done | bytes 135200 | tf_op jit(solution)/shard_map/ppermute | solution.py:182
  59.2 5.9 %collective-permute-done.3.far = bf16[528,128]{1,0:T(8,128)(2,1)S(1)} collective-permute-done((bf16[528,128]{1,0:T(8,128)(2,1)}, bf16[528,128]{1,0:T(8,128)(2,1)S(1)}, u32[]{:S(2)}, u32[]{:S(2)}) %collective-permute-start.3) | collective-permute-done | bytes 135200 | tf_op jit(solution)/shard_map/ppermute | solution.py:182
  65.1 3.9 %all-to-all-done.1.b = bf16[8,768,128]{2,1,0:T(8,128)(2,1)S(1)} async-done(((bf16[8,768,128]{2,1,0:T(8,128)(2,1)}), bf16[8,768,128]{2,1,0:T(8,128)(2,1)S(1)}, u32[]{:S(2)}, u32[]{:S(2)}) %all-to-all-start.1) | async-done | bytes 1572896 | tf_op jit(solution)/shard_map/all_to_all | solution.py:186
  69.0 0.0 copy-done.4
  69.0 0.0 copy-done.5
  69.0 1.2 %copy-done.1 = bf16[8,768,128]{2,1,0:T(8,128)(2,1)} copy-done((bf16[8,768,128]{2,1,0:T(8,128)(2,1)}, bf16[8,768,128]{2,1,0:T(8,128)(2,1)S(1)}, u32[]{:S(2)}) %copy-start.1) | copy-done | bytes 1572888
  70.2 12.4 %shard_map.107 = (bf16[512,512]{1,0:T(8,128)(2,1)}, bf16[512,512]{1,0:T(8,128)(2,1)}) custom-call(bf16[8,656,128]{2,1,0:T(8,128)(2,1)} %copy-done, bf16[8,768,128]{2,1,0:T(8,128)(2,1)} %copy-done.1, bf16[528,128]{1,0:T(8,128)(2,1)} %copy-done.4, bf16[528,128]{1,0:T(8,128)(2,1)} %copy-done.5, s32[1,64]{1,0:T(1,128)} %bitcast.4, f32[1,512]{1,0:T(1,128)} %bitcast.2), custom_call_target="tpu_custom_call" | custom-call | tf_op jit(solution)/shard_map/pallas_call | solution.py:199
  (7 shorter events, 0.0 us)
Async XLA Ops:
  4.7 4.4 %copy-start.6 = (bf16[8,128,128]{2,1,0:T(8,128)(2,1)S(1)}, bf16[8,128,128]{2,1,0:T(8,128)(2,1)}, u32[]{:S(2)}) copy-start(bf16[8,128,128]{2,1,0:T(8,128)(2,1)} %get-tuple-element.5) | copy-start | bytes 786436
  4.7 37.2 %all-to-all-start = ((bf16[8,656,128]{2,1,0:T(8,128)(2,1)}), bf16[8,656,128]{2,1,0:T(8,128)(2,1)S(1)}, u32[]{:S(2)}, u32[]{:S(2)}) async-start(bf16[8,656,128]{2,1,0:T(8,128)(2,1)} %get-tuple-element.4), calls=%async_computation | async-start | bytes 2686976 | tf_op jit(solution)/shard_map/all_to_all | solution.py:186
  9.1 15.8 %collective-permute-start = (bf16[8,128,128]{2,1,0:T(8,128)(2,1)S(1)}, bf16[8,128,128]{2,1,0:T(8,128)(2,1)S(1)}, u32[]{:S(2)}, u32[]{:S(2)}) collective-permute-start(bf16[8,128,128]{2,1,0:T(8,128)(2,1)S(1)} %copy-done.6), channel_id=1, source_target_pairs={{0,8},{8,16},{16,24},{24,32},{32,40},{40,48},{48,56},{56,64},{64,7... | collective-permute-start | bytes 786440 | tf_op jit(solution)/shard_map/ppermute | solution.py:182
  13.0 25.5 %collective-permute-start.1 = (bf16[8,128,128]{2,1,0:T(8,128)(2,1)S(1)}, bf16[8,128,128]{2,1,0:T(8,128)(2,1)S(1)}, u32[]{:S(2)}, u32[]{:S(2)}) collective-permute-start(bf16[8,128,128]{2,1,0:T(8,128)(2,1)S(1)} %copy-done.6), channel_id=1, source_target_pairs={{0,16},{8,24},{16,32},{24,40},{32,48},{40,56},{48,64},{56,72},{64,... | collective-permute-start | bytes 786440 | tf_op jit(solution)/shard_map/ppermute | solution.py:182
  24.9 13.5 %copy-start.2 = (bf16[8,128,128]{2,1,0:T(8,128)(2,1)}, bf16[8,128,128]{2,1,0:T(8,128)(2,1)S(1)}, u32[]{:S(2)}) copy-start(bf16[8,128,128]{2,1,0:T(8,128)(2,1)S(1)} %collective-permute-done.kv1) | copy-start | bytes 786436
  38.5 0.7 copy-start.3
  41.9 1.1 %copy-start = (bf16[8,656,128]{2,1,0:T(8,128)(2,1)}, bf16[8,656,128]{2,1,0:T(8,128)(2,1)S(1)}, u32[]{:S(2)}) copy-start(bf16[8,656,128]{2,1,0:T(8,128)(2,1)S(1)} %all-to-all-done.a) | copy-start | bytes 4030468
  43.0 26.0 %all-to-all-start.1 = ((bf16[8,768,128]{2,1,0:T(8,128)(2,1)}), bf16[8,768,128]{2,1,0:T(8,128)(2,1)S(1)}, u32[]{:S(2)}, u32[]{:S(2)}) async-start(bf16[8,768,128]{2,1,0:T(8,128)(2,1)} %shard_map.105), calls=%async_computation.1 | async-start | bytes 3145728 | tf_op jit(solution)/shard_map/all_to_all | solution.py:186
  50.7 8.5 %collective-permute-start.2 = (bf16[528,128]{1,0:T(8,128)(2,1)}, bf16[528,128]{1,0:T(8,128)(2,1)S(1)}, u32[]{:S(2)}, u32[]{:S(2)}) collective-permute-start(bf16[528,128]{1,0:T(8,128)(2,1)} %shard_map.106), channel_id=1, source_target_pairs={{0,8},{8,16},{16,24},{24,32},{32,40},{40,48},{48,56},{56,64},{64,7... | collective-permute-start | bytes 405512 | tf_op jit(solution)/shard_map/ppermute | solution.py:182
  52.6 12.4 %collective-permute-start.3 = (bf16[528,128]{1,0:T(8,128)(2,1)}, bf16[528,128]{1,0:T(8,128)(2,1)S(1)}, u32[]{:S(2)}, u32[]{:S(2)}) collective-permute-start(bf16[528,128]{1,0:T(8,128)(2,1)} %shard_map.106), channel_id=1, source_target_pairs={{0,16},{8,24},{16,32},{24,40},{32,48},{40,56},{48,64},{56,72},{64,... | collective-permute-start | bytes 405512 | tf_op jit(solution)/shard_map/ppermute | solution.py:182
  59.2 9.8 %copy-start.4 = (bf16[528,128]{1,0:T(8,128)(2,1)}, bf16[528,128]{1,0:T(8,128)(2,1)S(1)}, u32[]{:S(2)}) copy-start(bf16[528,128]{1,0:T(8,128)(2,1)S(1)} %collective-permute-done.2.near) | copy-start | bytes 405508
  65.1 3.9 %copy-start.5 = (bf16[528,128]{1,0:T(8,128)(2,1)}, bf16[528,128]{1,0:T(8,128)(2,1)S(1)}, u32[]{:S(2)}) copy-start(bf16[528,128]{1,0:T(8,128)(2,1)S(1)} %collective-permute-done.3.far) | copy-start | bytes 405508
  69.0 1.2 %copy-start.1 = (bf16[8,768,128]{2,1,0:T(8,128)(2,1)}, bf16[8,768,128]{2,1,0:T(8,128)(2,1)S(1)}, u32[]{:S(2)}) copy-start(bf16[8,768,128]{2,1,0:T(8,128)(2,1)S(1)} %all-to-all-done.1.b) | copy-start | bytes 4718596

commit v2 on v1

v2 whole, which is shorter than its diff:
```python
import math

import jax
import jax.numpy as jnp
from jax import lax
from jax.experimental import pallas as pl
from jax.experimental.pallas import tpu as pltpu
from jax.sharding import PartitionSpec as P

HEAD = 128
PEERS = 8
TOK = 64
HEADS = 4
BLOCK = PEERS * TOK
REACH = 2 * BLOCK
ROW_TILE = 128
LIN_TILE = 256
SPAN = REACH + ROW_TILE
DEC_ROW = 10 * TOK
ROWS_A = DEC_ROW + 16
ROWS_B = 10 * TOK
STATE_ROWS = HEADS * HEAD + 16
LOG2E = math.log2(math.e)
NEVER = -1e30
F32 = jnp.float32
BF16 = jnp.bfloat16
VMEM_LIMIT = 40 * 1024 * 1024


def silu(x):
    half = 0.5 * x.astype(F32)
    return (half + half * jnp.tanh(half)).astype(BF16)


def near_core(x):
    return pltpu.with_memory_space_constraint(x, pltpu.VMEM)


def call(body, out_shape, scratch=(), inputs=None):
    whole = pl.BlockSpec(memory_space=pltpu.VMEM)
    many = isinstance(out_shape, (tuple, list))
    return pl.pallas_call(
        body,
        out_shape=out_shape,
        **({} if inputs is None else dict(in_specs=inputs)),
        out_specs=tuple(whole for _ in out_shape) if many else whole,
        scratch_shapes=list(scratch),
        compiler_params=pltpu.CompilerParams(vmem_limit_bytes=VMEM_LIMIT),
    )


def columns(out, source, first, count):
    for peer in range(PEERS):
        for i in range(count):
            column = (peer * count + i) * HEAD
            out[peer, (first + i) * TOK : (first + i + 1) * TOK, :] = source[:, column : column + HEAD]


def pack_first(k, v, ak, av, decay, out, window, k_in, v_in, ak_in, av_in, decay_in, arrived):
    pairs = ((ak, ak_in), (av, av_in), (decay, decay_in), (k, k_in), (v, v_in))
    copies = [pltpu.make_async_copy(source, into, arrived.at[i]) for i, (source, into) in enumerate(pairs)]
    for copy in copies:
        copy.start()
    copies[0].wait()
    columns(out, ak_in, 8, 1)
    columns(window, ak_in, 0, 1)
    copies[1].wait()
    columns(out, av_in, 9, 1)
    columns(window, av_in, 1, 1)
    copies[2].wait()
    rows = jnp.concatenate([decay_in[...].astype(F32), jnp.zeros((32, 64), F32)], axis=1)
    for peer in range(PEERS):
        own = rows[HEADS * peer : HEADS * (peer + 1), :]
        own = jnp.concatenate([own, own, jnp.zeros((8, 128), F32)], axis=0)
        out[peer, DEC_ROW : DEC_ROW + 16, :] = own.astype(BF16)
    copies[3].wait()
    columns(out, k_in, 0, HEADS)
    copies[4].wait()
    columns(out, v_in, 4, HEADS)


def pack_second(q, aq, earlier, out):
    columns(out, aq, 4, HEADS)
    columns(out, q, 0, HEADS)
    out[:, 8 * TOK :, :] = earlier[...]


def begins(lens):
    start = lax.axis_index("ctx") * BLOCK
    lane = lax.broadcasted_iota(jnp.int32, (8, 128), 1)
    row = jnp.concatenate([lens[...], jnp.zeros((1, 64), jnp.int32)], axis=1)
    row = jnp.broadcast_to(row, (8, 128))
    total = row
    for step in (1, 2, 4, 8, 16, 32):
        total = total + jnp.where(lane >= step, pltpu.roll(total, step, 1), 0)
    first = (total - row)[0:1, :] - start
    first = jnp.where(lane[0:1, :] < 64, first, 1 << 20).astype(F32)
    place = lax.broadcasted_iota(jnp.int32, (BLOCK, 128), 0).astype(F32)
    return jnp.max(jnp.where(first <= place, first, -float(1 << 20)), axis=1, keepdims=True)


def decay_rows(a):
    source = lax.broadcasted_iota(jnp.int32, (128, 128), 0)
    place = lax.broadcasted_iota(jnp.int32, (128, 128), 1)
    low = jnp.where((source < TOK) & (source <= place), 1.0, 0.0).astype(BF16)
    high = jnp.where((source < TOK) & (source + TOK <= place), 1.0, 0.0).astype(BF16)
    before = jnp.zeros((16, 1), F32)
    parts = []
    for pair in range(PEERS // 2):
        part = jnp.dot(a[2 * pair, DEC_ROW : DEC_ROW + 16, :], low, preferred_element_type=F32)
        part += jnp.dot(a[2 * pair + 1, DEC_ROW : DEC_ROW + 16, :], high, preferred_element_type=F32)
        part += before
        before = part[:, 127:128]
        parts.append(part)
    return jnp.concatenate(parts, axis=1) * LOG2E


def gathered(a, index):
    return a[:, index * TOK : (index + 1) * TOK, :].reshape(BLOCK, HEAD)


def state(a, lens, out, all_out, cols, rows, maps):
    for index in range(2):
        all_out[STATE_ROWS + index * BLOCK : STATE_ROWS + (index + 1) * BLOCK, :] = gathered(a, 8 + index)
    begin = begins(lens)
    sums = decay_rows(a)
    rows[...] = sums
    turned = jnp.transpose(jnp.concatenate([sums, jnp.zeros((112, BLOCK), F32)], axis=0))
    lane = lax.broadcasted_iota(jnp.int32, (BLOCK, HEAD), 1)
    carry = jnp.where(begin < 0, jnp.exp2(-turned), 0.0)
    cols[...] = jnp.where(lane < HEADS, turned, jnp.where(lane == 8, begin, carry))
    last = begin[BLOCK - 1 : BLOCK, :]
    end = turned[BLOCK - 1 : BLOCK, :]
    place = lax.broadcasted_iota(jnp.int32, (BLOCK, 1), 0).astype(F32)
    weight = jnp.exp2(jnp.where(place >= last, turned - end, NEVER))
    extra = []
    for head in range(HEADS):
        key_map = silu(gathered(a, head))
        maps[head * BLOCK : (head + 1) * BLOCK, :] = key_map
        end_keys = (key_map.astype(F32) * weight[:, head : head + 1]).astype(BF16)
        total = lax.dot_general(
            end_keys, gathered(a, 4 + head), (((0,), (0,)), ((), ())), preferred_element_type=F32
        )
        out[head * HEAD : (head + 1) * HEAD, :] = total.astype(BF16)
        all_out[head * HEAD : (head + 1) * HEAD, :] = total.astype(BF16)
        gone = jnp.where(last < 0, jnp.exp2(-end[:, head : head + 1]), 0.0)
        extra.append(jnp.broadcast_to(gone, (1, HEAD)))
    decay = jnp.concatenate([*extra, jnp.zeros((4, HEAD), F32)], axis=0)
    high = decay.astype(BF16).astype(F32)
    parts = jnp.concatenate([high, decay - high], axis=0).astype(BF16)
    out[HEADS * HEAD :, :] = parts
    all_out[HEADS * HEAD : STATE_ROWS, :] = parts


def attention(a, b, near, cols, att_out, keys, values, bias):
    values[:, HEAD:] = jnp.ones((3 * BLOCK, HEAD), BF16)
    for index, ref in enumerate((keys, values)):
        ref[:BLOCK, :HEAD] = gathered(b, 8 + index)
        ref[BLOCK : 2 * BLOCK, :HEAD] = near[STATE_ROWS + index * BLOCK : STATE_ROWS + (index + 1) * BLOCK, :]
        ref[2 * BLOCK :, :HEAD] = gathered(a, 8 + index)
    source = (lax.broadcasted_iota(jnp.int32, (ROW_TILE, SPAN), 1) - REACH).astype(F32)
    place = lax.broadcasted_iota(jnp.int32, (ROW_TILE, SPAN), 0).astype(F32)
    for tile in range(BLOCK // ROW_TILE):
        at = slice(tile * ROW_TILE, (tile + 1) * ROW_TILE)
        span = slice(tile * ROW_TILE, tile * ROW_TILE + SPAN)
        begin = cols[at, 8:9] - float(tile * ROW_TILE)
        bias[...] = jnp.where((source <= place) & (source >= begin), 0.0, NEVER)
        for head in range(HEADS):
            query = b[2 * tile : 2 * tile + 2, (4 + head) * TOK : (5 + head) * TOK, :].reshape(ROW_TILE, HEAD)
            scores = lax.dot_general(
                query, keys[span, :], (((1,), (1,)), ((), ())), preferred_element_type=F32
            )
            scores = scores * (HEAD ** -0.5 * LOG2E) + bias[...]
            weights = jnp.exp2(scores - jnp.max(scores, axis=1, keepdims=True)).astype(BF16)
            mixed = jnp.dot(weights, values[span, :], preferred_element_type=F32)
            att_out[at, head * HEAD : (head + 1) * HEAD] = (mixed[:, :HEAD] / mixed[:, HEAD:]).astype(BF16)


def lightning(a, b, near, far, cols, rows, maps, gain, lin_out, queries, incoming):
    shrink = near[HEADS * HEAD : STATE_ROWS, :].astype(F32)
    shrink = shrink[0:8, :] + shrink[8:16, :]
    pieces = [slice(head * HEAD, (head + 1) * HEAD) for head in range(HEADS)]
    for head, piece in enumerate(pieces):
        queries[head * BLOCK : (head + 1) * BLOCK, :] = silu(gathered(b, head))
        both = near[piece, :].astype(F32) + shrink[head : head + 1, :] * far[piece, :].astype(F32)
        incoming[piece, :] = both.astype(BF16)
    for tile in range(BLOCK // LIN_TILE):
        at = slice(tile * LIN_TILE, (tile + 1) * LIN_TILE)
        width = (tile + 1) * LIN_TILE
        peers = width // TOK
        source = lax.broadcasted_iota(jnp.int32, (LIN_TILE, width), 1).astype(F32)
        place = lax.broadcasted_iota(jnp.int32, (LIN_TILE, width), 0).astype(F32) + float(tile * LIN_TILE)
        bias = jnp.where((source <= place) & (source >= cols[at, 8:9]), 0.0, NEVER)
        query = [queries[head * BLOCK + tile * LIN_TILE : head * BLOCK + width, :] for head in range(HEADS)]
        carried = [jnp.dot(query[h], incoming[pieces[h], :], preferred_element_type=F32) for h in range(HEADS)]
        scores = [
            lax.dot_general(
                query[h],
                maps[h * BLOCK : h * BLOCK + width, :],
                (((1,), (1,)), ((), ())),
                preferred_element_type=F32,
            )
            for h in range(HEADS)
        ]
        gaps = [(rows[h : h + 1, :width] - cols[at, h : h + 1]) + bias for h in range(HEADS)]
        weighted = [(jnp.exp2(gaps[h]) * scores[h]).astype(BF16) for h in range(HEADS)]
        inside = [
            jnp.dot(
                weighted[h],
                a[:peers, (4 + h) * TOK : (5 + h) * TOK, :].reshape(width, HEAD),
                preferred_element_type=F32,
            )
            for h in range(HEADS)
        ]
        for h, piece in enumerate(pieces):
            combined = inside[h] + carried[h] * cols[at, 4 + h : 5 + h]
            mean = jnp.mean(combined * combined, axis=1, keepdims=True)
            lin_out[at, piece] = (combined * lax.rsqrt(mean + 1e-6) * gain[:, piece]).astype(BF16)


def shifted(block, distance):
    count = lax.axis_size("ctx")
    return lax.ppermute(block, "ctx", [(i, i + distance) for i in range(count - distance)])


def exchanged(packed):
    return lax.all_to_all(packed, "uly", split_axis=0, concat_axis=0, tiled=True)


def shards(q, k, v, decay, gain, lens, aq, ak, av):
    lens = lens.reshape(1, 64)
    fast = lambda dtype, *dims: pltpu.VMEM(dims, dtype)
    shape = lambda *dims: jax.ShapeDtypeStruct(dims, BF16)
    first, window = call(
        pack_first,
        (fast(BF16, PEERS, ROWS_A, HEAD), fast(BF16, PEERS, 2 * TOK, HEAD)),
        [
            pltpu.VMEM((TOK, PEERS * HEADS * HEAD), BF16),
            pltpu.VMEM((TOK, PEERS * HEADS * HEAD), BF16),
            pltpu.VMEM((TOK, PEERS * HEAD), BF16),
            pltpu.VMEM((TOK, PEERS * HEAD), BF16),
            pltpu.VMEM((PEERS * HEADS, TOK), BF16),
            pltpu.SemaphoreType.DMA((5,)),
        ],
        [pl.BlockSpec(memory_space=pltpu.HBM)] * 5,
    )(*(pltpu.with_memory_space_constraint(x, pltpu.HBM) for x in (k, v, ak, av, decay.T)))
    a = near_core(exchanged(first))
    earlier = shifted(window, 2)
    b = near_core(exchanged(call(pack_second, fast(BF16, PEERS, ROWS_B, HEAD))(q, aq, near_core(earlier))))
    own, all_own, cols, rows, maps = call(
        state,
        (
            fast(BF16, STATE_ROWS, HEAD),
            fast(BF16, STATE_ROWS + 2 * BLOCK, HEAD),
            fast(F32, BLOCK, HEAD),
            fast(F32, 16, BLOCK),
            fast(BF16, HEADS * BLOCK, HEAD),
        ),
    )(a, lens)
    near, far = shifted(all_own, 1), shifted(own, 2)
    att_out = call(
        attention,
        shape(BLOCK, HEADS * HEAD),
        [
            pltpu.VMEM((3 * BLOCK, HEAD), BF16),
            pltpu.VMEM((3 * BLOCK, 2 * HEAD), BF16),
            pltpu.VMEM((ROW_TILE, SPAN), F32),
        ],
    )(a, b, near_core(near), near_core(cols))
    lin_out = call(
        lightning,
        shape(BLOCK, HEADS * HEAD),
        [pltpu.VMEM((HEADS * BLOCK, HEAD), BF16), pltpu.VMEM((HEADS * HEAD, HEAD), BF16)],
    )(
        a,
        b,
        near_core(near),
        near_core(far),
        near_core(cols),
        near_core(rows),
        near_core(maps),
        gain.reshape(1, HEADS * HEAD),
    )
    return lin_out, att_out


def solution(mesh):
    rows = P(("ctx", "uly"), None)
    return jax.shard_map(
        shards,
        mesh=mesh,
        in_specs=(rows, rows, rows, rows, P("uly"), P(), rows, rows, rows),
        out_specs=(P("ctx", "uly"), P("ctx", "uly")),
        check_vma=False,
    )
```

time: 83 us -> 64.5 us (0.78)
  Pallas kernels: 21.1 us -> 13 us
  waiting for transfers between devices: 33.5 us -> 29.5 us
  starting transfers between devices: 22.9 us -> 19.1 us
  local copies, waits for them, and re-layouts: 4.34 us -> 1.88 us
    ppermute x4 -> x3, waiting for transfers between devices: 29.6 us -> 18.5 us  [shifted(): lax.ppermute(block, 'ctx', [(i, i + distance) for i in range(count - dist...]
    pallas_call x4 -> x5, Pallas kernels: 21.1 us -> 13 us  [the longest x1 5.01 us: shards(): call(attention, shape(BLOCK, HEADS * HEAD), [pltpu.VMEM((3 * BLOCK, HEAD)...]
    all_to_all x2, waiting for transfers between devices: 3.91 us -> 11 us  [exchanged(): lax.all_to_all(packed, 'uly', split_axis=0, concat_axis=0, tiled=True)]
    ppermute x4 -> x3, starting transfers between devices: 14 us -> 10 us  [shifted(): lax.ppermute(block, 'ctx', [(i, i + distance) for i in range(count - dist...]
    unnamed x15 -> x14, local copies, waits for them, and re-layouts: 4.34 us -> 1.88 us
  transfers between devices with their start and end apart: 6 -> 5, of which waited for: 5 -> 2; matrix products, arithmetic and copies ran while one was open for 0% -> 0% of each run, Pallas kernels for 7% -> 11%
where the time goes in v2:
time: 64.5 us; the launch traced here: 64.2 us
  waiting for transfers between devices  29.5 us (46%)
  starting transfers between devices  19.1 us (30%)
  Pallas kernels  13 us (20%)
  local copies, waits for them, and re-layouts  1.88 us (3%)
  between operations  0.71 us (1%)
    ppermute x3, waiting for transfers between devices, shifted(): lax.ppermute(block, 'ctx', [(i, i + distance) for i in range(count - dist...  18.5 us
    all_to_all x2, waiting for transfers between devices, exchanged(): lax.all_to_all(packed, 'uly', split_axis=0, concat_axis=0, tiled=True)  11 us
    ppermute x3, starting transfers between devices, shifted(): lax.ppermute(block, 'ctx', [(i, i + distance) for i in range(count - dist...  10 us
    all_to_all x2, starting transfers between devices, exchanged(): lax.all_to_all(packed, 'uly', split_axis=0, concat_axis=0, tiled=True)  9.02 us
    pallas_call x1, Pallas kernels, shards(): call(attention, shape(BLOCK, HEADS * HEAD), [pltpu.VMEM((3 * BLOCK, HEAD)...  5.01 us
    pallas_call x1, Pallas kernels, shards(): call(lightning, shape(BLOCK, HEADS * HEAD), [pltpu.VMEM((HEADS * BLOCK, H...  3.14 us
    pallas_call x1, Pallas kernels, shards(): call(pack_first, (fast(BF16, PEERS, ROWS_A, HEAD), fast(BF16, PEERS, 2 *...  2.58 us
    pallas_call x1, Pallas kernels, shards(): call(state, (fast(BF16, STATE_ROWS, HEAD), fast(BF16, STATE_ROWS + 2 * BL...  2.12 us
  transfers between devices with their start and end apart: 5, of which 2 were waited for; matrix products, arithmetic and copies ran while one was open for 0% of the time, Pallas kernels for 11%

profile of v2, /device:TPU:56, one launch (start us, length us, event | category | flops | bytes accessed | tf_op | source)
XLA Modules:
  0.0 64.2 jit_solution(463606338425109868)
XLA Ops:
  0.6 2.6 %shard_map.104 = (bf16[8,656,128]{2,1,0:T(8,128)(2,1)}, bf16[8,128,128]{2,1,0:T(8,128)(2,1)S(1)}) custom-call(bf16[64,4096]{1,0:T(8,128)(2,1)} %k.1, bf16[64,4096]{1,0:T(8,128)(2,1)} %v.1, bf16[64,1024]{1,0:T(8,128)(2,1)} %ak.1, bf16[64,1024]{1,0:T(8,128)(2,1)} %av.1, bf16[32,64]{1,0:T(8,128)(2,1)} %bitcast.5), custom_call_target="tpu_custom_call" | custom-call | tf_op jit(solution)/shard_map/pallas_call | solution.py:234
  3.2 0.0 copy-start.1
  3.2 0.0 copy-start.2
  3.2 4.4 %all-to-all-start = ((bf16[8,656,128]{2,1,0:T(8,128)(2,1)}), bf16[8,656,128]{2,1,0:T(8,128)(2,1)S(1)}, u32[]{:S(2)}, u32[]{:S(2)}) async-start(bf16[8,656,128]{2,1,0:T(8,128)(2,1)} %get-tuple-element.9), calls=%async_computation | async-start | bytes 2686976 | tf_op jit(solution)/shard_map/all_to_all | solution.py:227
  7.7 5.2 %collective-permute-start = (bf16[8,128,128]{2,1,0:T(8,128)(2,1)S(1)}, bf16[8,128,128]{2,1,0:T(8,128)(2,1)S(1)}, u32[]{:S(2)}, u32[]{:S(2)}) collective-permute-start(bf16[8,128,128]{2,1,0:T(8,128)(2,1)S(1)} %get-tuple-element.10), channel_id=1, source_target_pairs={{0,16},{8,24},{16,32},{24,40},{32,48},{40,56},{48,64},{56,72},{64,... | collective-permute-start | bytes 786440 | tf_op jit(solution)/shard_map/ppermute | solution.py:223
  12.9 18.5 %collective-permute-done.earlier = bf16[8,128,128]{2,1,0:T(8,128)(2,1)S(1)} collective-permute-done((bf16[8,128,128]{2,1,0:T(8,128)(2,1)S(1)}, bf16[8,128,128]{2,1,0:T(8,128)(2,1)S(1)}, u32[]{:S(2)}, u32[]{:S(2)}) %collective-permute-start) | collective-permute-done | bytes 262176 | tf_op jit(solution)/shard_map/ppermute | solution.py:223
  31.4 0.0 copy-done.1
  31.4 0.0 copy-done.2
  31.4 0.2 shard_map.105
  31.6 0.0 copy-start
  31.6 1.1 %copy-done = bf16[8,640,128]{2,1,0:T(8,128)(2,1)} copy-done((bf16[8,640,128]{2,1,0:T(8,128)(2,1)}, bf16[8,640,128]{2,1,0:T(8,128)(2,1)S(1)}, u32[]{:S(2)}) %copy-start) | copy-done | bytes 1310744
  32.7 0.0 all-to-all-done.a
  32.7 4.6 %all-to-all-start.1 = ((bf16[8,640,128]{2,1,0:T(8,128)(2,1)}), bf16[8,640,128]{2,1,0:T(8,128)(2,1)S(1)}, u32[]{:S(2)}, u32[]{:S(2)}) async-start(bf16[8,640,128]{2,1,0:T(8,128)(2,1)} %copy-done), calls=%async_computation.1 | async-start | bytes 2621440 | tf_op jit(solution)/shard_map/all_to_all | solution.py:227
  37.3 0.0 copy-done.6
  37.3 2.1 %shard_map.106 = (bf16[528,128]{1,0:T(8,128)(2,1)}, bf16[1552,128]{1,0:T(8,128)(2,1)}, f32[512,128]{1,0:T(8,128)S(1)}, f32[16,512]{1,0:T(8,128)S(1)}, bf16[2048,128]{1,0:T(8,128)(2,1)S(1)}) custom-call(bf16[8,656,128]{2,1,0:T(8,128)(2,1)S(1)} %all-to-all-done.a, s32[1,64]{1,0:T(1,128)S(1)} %bitcast.4), custom_call_target="tpu_custom_call" | custom-call | tf_op jit(solution)/shard_map/pallas_call | solution.py:250
  39.4 0.8 %copy-done.3 = bf16[2048,128]{1,0:T(8,128)(2,1)} copy-done((bf16[2048,128]{1,0:T(8,128)(2,1)}, bf16[2048,128]{1,0:T(8,128)(2,1)S(1)}, u32[]{:S(2)}) %copy-start.3) | copy-done | bytes 524312
  40.2 1.9 %collective-permute-start.1 = (bf16[1552,128]{1,0:T(8,128)(2,1)}, bf16[1552,128]{1,0:T(8,128)(2,1)S(1)}, u32[]{:S(2)}, u32[]{:S(2)}) collective-permute-start(bf16[1552,128]{1,0:T(8,128)(2,1)} %get-tuple-element.11), channel_id=1, source_target_pairs={{0,8},{8,16},{16,24},{24,32},{32,40},{40,48},{48,56},{56,64},{64,7... | collective-permute-start | bytes 1191944 | tf_op jit(solution)/shard_map/ppermute | solution.py:223
  42.1 3.0 %collective-permute-start.2 = (bf16[528,128]{1,0:T(8,128)(2,1)}, bf16[528,128]{1,0:T(8,128)(2,1)S(1)}, u32[]{:S(2)}, u32[]{:S(2)}) collective-permute-start(bf16[528,128]{1,0:T(8,128)(2,1)} %get-tuple-element.12), channel_id=1, source_target_pairs={{0,16},{8,24},{16,32},{24,40},{32,48},{40,56},{48,64},{56,72},{64,... | collective-permute-start | bytes 405512 | tf_op jit(solution)/shard_map/ppermute | solution.py:223
  45.1 11.0 %all-to-all-done.1.b = bf16[8,640,128]{2,1,0:T(8,128)(2,1)S(1)} async-done(((bf16[8,640,128]{2,1,0:T(8,128)(2,1)}), bf16[8,640,128]{2,1,0:T(8,128)(2,1)S(1)}, u32[]{:S(2)}, u32[]{:S(2)}) %all-to-all-start.1) | async-done | bytes 1310752 | tf_op jit(solution)/shard_map/all_to_all | solution.py:227
  56.0 0.0 collective-permute-done.1.near
  56.0 5.0 %shard_map.108 = bf16[512,512]{1,0:T(8,128)(2,1)} custom-call(bf16[8,656,128]{2,1,0:T(8,128)(2,1)S(1)} %all-to-all-done.a, bf16[8,640,128]{2,1,0:T(8,128)(2,1)S(1)} %all-to-all-done.1.b, bf16[1552,128]{1,0:T(8,128)(2,1)S(1)} %collective-permute-done.1.near, f32[512,128]{1,0:T(8,128)S(1)} %get-tuple-element.13.cols), custom_call_target="tpu_custom_call" | custom-call | tf_op jit(solution)/shard_map/pallas_call | solution.py:261
  61.0 0.0 collective-permute-done.2.far
  61.1 0.0 copy-done.4
  61.1 3.1 %shard_map.107 = bf16[512,512]{1,0:T(8,128)(2,1)} custom-call(bf16[8,656,128]{2,1,0:T(8,128)(2,1)S(1)} %all-to-all-done.a, bf16[8,640,128]{2,1,0:T(8,128)(2,1)S(1)} %all-to-all-done.1.b, bf16[1552,128]{1,0:T(8,128)(2,1)S(1)} %collective-permute-done.1.near, bf16[528,128]{1,0:T(8,128)(2,1)S(1)} %collective-permute-done.2.far, ...), custom_call_target="tpu_custom_call" | custom-call | tf_op jit(solution)/shard_map/pallas_call | solution.py:270
  (5 shorter events, 0.0 us)
Async XLA Ops:
  3.2 28.2 %copy-start.1 = (bf16[64,4096]{1,0:T(8,128)(2,1)S(1)}, bf16[64,4096]{1,0:T(8,128)(2,1)}, u32[]{:S(2)}) copy-start(bf16[64,4096]{1,0:T(8,128)(2,1)} %q.1) | copy-start | bytes 1572868
  3.2 28.2 %copy-start.2 = (bf16[64,4096]{1,0:T(8,128)(2,1)S(1)}, bf16[64,4096]{1,0:T(8,128)(2,1)}, u32[]{:S(2)}) copy-start(bf16[64,4096]{1,0:T(8,128)(2,1)} %aq.1) | copy-start | bytes 1572868
  3.2 29.4 %all-to-all-start = ((bf16[8,656,128]{2,1,0:T(8,128)(2,1)}), bf16[8,656,128]{2,1,0:T(8,128)(2,1)S(1)}, u32[]{:S(2)}, u32[]{:S(2)}) async-start(bf16[8,656,128]{2,1,0:T(8,128)(2,1)} %get-tuple-element.9), calls=%async_computation | async-start | bytes 2686976 | tf_op jit(solution)/shard_map/all_to_all | solution.py:227
  7.7 23.7 %collective-permute-start = (bf16[8,128,128]{2,1,0:T(8,128)(2,1)S(1)}, bf16[8,128,128]{2,1,0:T(8,128)(2,1)S(1)}, u32[]{:S(2)}, u32[]{:S(2)}) collective-permute-start(bf16[8,128,128]{2,1,0:T(8,128)(2,1)S(1)} %get-tuple-element.10), channel_id=1, source_target_pairs={{0,16},{8,24},{16,32},{24,40},{32,48},{40,56},{48,64},{56,72},{64,... | collective-permute-start | bytes 786440 | tf_op jit(solution)/shard_map/ppermute | solution.py:223
  31.6 1.1 %copy-start = (bf16[8,640,128]{2,1,0:T(8,128)(2,1)}, bf16[8,640,128]{2,1,0:T(8,128)(2,1)S(1)}, u32[]{:S(2)}) copy-start(bf16[8,640,128]{2,1,0:T(8,128)(2,1)S(1)} %shard_map.105) | copy-start | bytes 3932164
  32.7 4.6 %copy-start.6 = (s32[64]{0:T(128)S(1)}, s32[64]{0:T(128)}, u32[]{:S(2)}) copy-start(s32[64]{0:T(128)} %param.14) | copy-start | bytes 772
  32.7 23.4 %all-to-all-start.1 = ((bf16[8,640,128]{2,1,0:T(8,128)(2,1)}), bf16[8,640,128]{2,1,0:T(8,128)(2,1)S(1)}, u32[]{:S(2)}, u32[]{:S(2)}) async-start(bf16[8,640,128]{2,1,0:T(8,128)(2,1)} %copy-done), calls=%async_computation.1 | async-start | bytes 2621440 | tf_op jit(solution)/shard_map/all_to_all | solution.py:227
  39.4 0.8 %copy-start.3 = (bf16[2048,128]{1,0:T(8,128)(2,1)}, bf16[2048,128]{1,0:T(8,128)(2,1)S(1)}, u32[]{:S(2)}) copy-start(bf16[2048,128]{1,0:T(8,128)(2,1)S(1)} %get-tuple-element.15.maps) | copy-start | bytes 1572868
  40.2 15.9 %collective-permute-start.1 = (bf16[1552,128]{1,0:T(8,128)(2,1)}, bf16[1552,128]{1,0:T(8,128)(2,1)S(1)}, u32[]{:S(2)}, u32[]{:S(2)}) collective-permute-start(bf16[1552,128]{1,0:T(8,128)(2,1)} %get-tuple-element.11), channel_id=1, source_target_pairs={{0,8},{8,16},{16,24},{24,32},{32,40},{40,48},{48,56},{56,64},{64,7... | collective-permute-start | bytes 1191944 | tf_op jit(solution)/shard_map/ppermute | solution.py:223
  42.1 19.0 %collective-permute-start.2 = (bf16[528,128]{1,0:T(8,128)(2,1)}, bf16[528,128]{1,0:T(8,128)(2,1)S(1)}, u32[]{:S(2)}, u32[]{:S(2)}) collective-permute-start(bf16[528,128]{1,0:T(8,128)(2,1)} %get-tuple-element.12), channel_id=1, source_target_pairs={{0,16},{8,24},{16,32},{24,40},{32,48},{40,56},{48,64},{56,72},{64,... | collective-permute-start | bytes 405512 | tf_op jit(solution)/shard_map/ppermute | solution.py:223
  56.0 5.0 %copy-start.4 = (bf16[2048,128]{1,0:T(8,128)(2,1)S(1)}, bf16[2048,128]{1,0:T(8,128)(2,1)}, u32[]{:S(2)}) copy-start(bf16[2048,128]{1,0:T(8,128)(2,1)} %copy-done.3) | copy-start | bytes 1572868
  56.0 5.0 %copy-start.5 = (f32[512]{0:T(512)S(1)}, f32[512]{0:T(512)}, u32[]{:S(2)}) copy-start(f32[512]{0:T(512)} %param.13) | copy-start | bytes 6148

commit v3 on v2

v3 whole, which is shorter than its diff:
```python
import math

import jax
import jax.numpy as jnp
from jax import lax
from jax.experimental import pallas as pl
from jax.experimental.pallas import tpu as pltpu
from jax.sharding import PartitionSpec as P

HEAD = 128
PEERS = 8
TOK = 64
HEADS = 4
BLOCK = PEERS * TOK
REACH = 2 * BLOCK
ROW_TILE = 128
LIN_TILE = 256
PART = BLOCK + ROW_TILE
DEC_ROW = 10 * TOK
ROWS_A = DEC_ROW + 16
ROWS_B = 10 * TOK
STATE_ROWS = HEADS * HEAD + 16
LOG2E = math.log2(math.e)
NEVER = -1e30
SCALE = HEAD ** -0.5 * LOG2E
F32 = jnp.float32
BF16 = jnp.bfloat16
VMEM_LIMIT = 24 * 1024 * 1024


def silu(x):
    half = 0.5 * x.astype(F32)
    return (half + half * jnp.tanh(half)).astype(BF16)


def near_core(x):
    return pltpu.with_memory_space_constraint(x, pltpu.VMEM)


def call(body, out_shape, scratch=(), inputs=None, output=pl.BlockSpec(memory_space=pltpu.VMEM)):
    many = isinstance(out_shape, (tuple, list))
    return pl.pallas_call(
        body,
        out_shape=out_shape,
        **({} if inputs is None else dict(in_specs=inputs)),
        out_specs=tuple(output for _ in out_shape) if many else output,
        scratch_shapes=list(scratch),
        compiler_params=pltpu.CompilerParams(vmem_limit_bytes=VMEM_LIMIT),
    )


def columns(out, source, first, count):
    for peer in range(PEERS):
        for i in range(count):
            column = (peer * count + i) * HEAD
            out[peer, (first + i) * TOK : (first + i + 1) * TOK, :] = source[:, column : column + HEAD]


def pack_first(k, v, ak, av, decay, out, window, k_in, v_in, ak_in, av_in, decay_in, staged, raw, arrived, left):
    pairs = ((ak, ak_in), (av, av_in), (decay, decay_in), (k, k_in), (v, v_in))
    copies = [pltpu.make_async_copy(source, into, arrived.at[i]) for i, (source, into) in enumerate(pairs)]
    for copy in copies:
        copy.start()
    parts = [slice(8 * TOK, ROWS_A), slice(0, 4 * TOK), slice(4 * TOK, 8 * TOK)]
    away = [pltpu.make_async_copy(staged.at[:, part], out.at[:, part], left.at[i]) for i, part in enumerate(parts)]
    away.append(pltpu.make_async_copy(raw, window, left.at[3]))
    copies[0].wait()
    columns(staged, ak_in, 8, 1)
    columns(raw, ak_in, 0, 1)
    copies[1].wait()
    columns(staged, av_in, 9, 1)
    columns(raw, av_in, 1, 1)
    copies[2].wait()
    rows = jnp.concatenate([decay_in[...].astype(F32), jnp.zeros((32, 64), F32)], axis=1)
    for peer in range(PEERS):
        own = rows[HEADS * peer : HEADS * (peer + 1), :]
        own = jnp.concatenate([own, own, jnp.zeros((8, 128), F32)], axis=0)
        staged[peer, DEC_ROW : DEC_ROW + 16, :] = own.astype(BF16)
    away[0].start()
    away[3].start()
    copies[3].wait()
    columns(staged, k_in, 0, HEADS)
    away[1].start()
    copies[4].wait()
    columns(staged, v_in, 4, HEADS)
    away[2].start()
    for copy in away:
        copy.wait()


def pack_second(q, aq, out):
    columns(out, aq, 4, HEADS)
    columns(out, q, 0, HEADS)


def pack_body(q, aq, out, staged, done):
    pack_second(q, aq, staged)
    copy = pltpu.make_async_copy(staged, out.at[:, : 8 * TOK, :], done)
    copy.start()
    copy.wait()


def insert(earlier, packed, out, done):
    copy = pltpu.make_async_copy(earlier, out.at[:, 8 * TOK :, :], done)
    copy.start()
    copy.wait()


def begins(lens):
    start = lax.axis_index("ctx") * BLOCK
    lane = lax.broadcasted_iota(jnp.int32, (8, 128), 1)
    row = jnp.concatenate([lens[...], jnp.zeros((1, 64), jnp.int32)], axis=1)
    row = jnp.broadcast_to(row, (8, 128))
    total = row
    for step in (1, 2, 4, 8, 16, 32):
        total = total + jnp.where(lane >= step, pltpu.roll(total, step, 1), 0)
    first = (total - row)[0:1, :] - start
    first = jnp.where(lane[0:1, :] < 64, first, 1 << 20).astype(F32)
    place = lax.broadcasted_iota(jnp.int32, (BLOCK, 128), 0).astype(F32)
    return jnp.max(jnp.where(first <= place, first, -float(1 << 20)), axis=1, keepdims=True)


def decay_rows(a):
    source = lax.broadcasted_iota(jnp.int32, (128, 128), 0)
    place = lax.broadcasted_iota(jnp.int32, (128, 128), 1)
    low = jnp.where((source < TOK) & (source <= place), 1.0, 0.0).astype(BF16)
    high = jnp.where((source < TOK) & (source + TOK <= place), 1.0, 0.0).astype(BF16)
    before = jnp.zeros((16, 1), F32)
    parts = []
    for pair in range(PEERS // 2):
        part = jnp.dot(a[2 * pair, DEC_ROW : DEC_ROW + 16, :], low, preferred_element_type=F32)
        part += jnp.dot(a[2 * pair + 1, DEC_ROW : DEC_ROW + 16, :], high, preferred_element_type=F32)
        part += before
        before = part[:, 127:128]
        parts.append(part)
    return jnp.concatenate(parts, axis=1) * LOG2E


def gathered(a, index):
    return a[:, index * TOK : (index + 1) * TOK, :].reshape(BLOCK, HEAD)


def state(a, lens, out, all_out, cols, rows):
    for index in range(2):
        all_out[STATE_ROWS + index * BLOCK : STATE_ROWS + (index + 1) * BLOCK, :] = gathered(a, 8 + index)
    begin = begins(lens)
    sums = decay_rows(a)
    rows[...] = sums
    turned = jnp.transpose(jnp.concatenate([sums, jnp.zeros((112, BLOCK), F32)], axis=0))
    lane = lax.broadcasted_iota(jnp.int32, (BLOCK, HEAD), 1)
    carry = jnp.where(begin < 0, jnp.exp2(-turned), 0.0)
    cols[...] = jnp.where(lane < HEADS, turned, jnp.where(lane == 8, begin, carry))
    last = begin[BLOCK - 1 : BLOCK, :]
    end = turned[BLOCK - 1 : BLOCK, :]
    place = lax.broadcasted_iota(jnp.int32, (BLOCK, 1), 0).astype(F32)
    weight = jnp.exp2(jnp.where(place >= last, turned - end, NEVER))
    extra = []
    for head in range(HEADS):
        key_map = silu(gathered(a, head))
        end_keys = (key_map.astype(F32) * weight[:, head : head + 1]).astype(BF16)
        total = lax.dot_general(
            end_keys, gathered(a, 4 + head), (((0,), (0,)), ((), ())), preferred_element_type=F32
        )
        out[head * HEAD : (head + 1) * HEAD, :] = total.astype(BF16)
        all_out[head * HEAD : (head + 1) * HEAD, :] = total.astype(BF16)
        gone = jnp.where(last < 0, jnp.exp2(-end[:, head : head + 1]), 0.0)
        extra.append(jnp.broadcast_to(gone, (1, HEAD)))
    decay = jnp.concatenate([*extra, jnp.zeros((4, HEAD), F32)], axis=0)
    high = decay.astype(BF16).astype(F32)
    parts = jnp.concatenate([high, decay - high], axis=0).astype(BF16)
    out[HEADS * HEAD :, :] = parts
    all_out[HEADS * HEAD : STATE_ROWS, :] = parts


def within(a, b, cols, rows, mixed_out, highest_out, inside_out, queries, keys, values, bias, maps):
    values[:, HEAD:] = jnp.ones((2 * BLOCK, HEAD), BF16)
    for index, ref in enumerate((keys, values)):
        ref[:BLOCK, :HEAD] = gathered(b, 8 + index)
        ref[BLOCK:, :HEAD] = gathered(a, 8 + index)
    lane = lax.broadcasted_iota(jnp.int32, (ROW_TILE, PART), 1)
    place = lax.broadcasted_iota(jnp.int32, (ROW_TILE, PART), 0).astype(F32)
    for tile in range(BLOCK // ROW_TILE):
        at = slice(tile * ROW_TILE, (tile + 1) * ROW_TILE)
        span = slice(tile * ROW_TILE, tile * ROW_TILE + PART)
        begin = cols[at, 8:9] - float(tile * ROW_TILE)
        source = jnp.where(lane < BLOCK - tile * ROW_TILE, lane - REACH, lane - BLOCK).astype(F32)
        bias[...] = jnp.where((source <= place) & (source >= begin), 0.0, NEVER)
        for head in range(HEADS):
            query = b[2 * tile : 2 * tile + 2, (4 + head) * TOK : (5 + head) * TOK, :].reshape(ROW_TILE, HEAD)
            scores = lax.dot_general(
                query, keys[span, :], (((1,), (1,)), ((), ())), preferred_element_type=F32
            )
            scores = scores * SCALE + bias[...]
            highest = jnp.max(scores, axis=1, keepdims=True)
            weights = jnp.exp2(scores - highest).astype(BF16)
            mixed_out[at, 2 * head * HEAD : 2 * (head + 1) * HEAD] = jnp.dot(
                weights, values[span, :], preferred_element_type=F32
            )
            highest_out[at, head * HEAD : (head + 1) * HEAD] = jnp.broadcast_to(highest, (ROW_TILE, HEAD))

    for head in range(HEADS):
        queries[head * BLOCK : (head + 1) * BLOCK, :] = silu(gathered(b, head))
        maps[head * BLOCK : (head + 1) * BLOCK, :] = silu(gathered(a, head))
    for tile in range(BLOCK // LIN_TILE):
        at = slice(tile * LIN_TILE, (tile + 1) * LIN_TILE)
        width = (tile + 1) * LIN_TILE
        peers = width // TOK
        source = lax.broadcasted_iota(jnp.int32, (LIN_TILE, width), 1).astype(F32)
        place = lax.broadcasted_iota(jnp.int32, (LIN_TILE, width), 0).astype(F32) + float(tile * LIN_TILE)
        allowed = jnp.where((source <= place) & (source >= cols[at, 8:9]), 0.0, NEVER)
        scores = [
            lax.dot_general(
                queries[h * BLOCK + tile * LIN_TILE : h * BLOCK + width, :],
                maps[h * BLOCK : h * BLOCK + width, :],
                (((1,), (1,)), ((), ())),
                preferred_element_type=F32,
            )
            for h in range(HEADS)
        ]
        gaps = [(rows[h : h + 1, :width] - cols[at, h : h + 1]) + allowed for h in range(HEADS)]
        weighted = [(jnp.exp2(gaps[h]) * scores[h]).astype(BF16) for h in range(HEADS)]
        for h in range(HEADS):
            inside_out[at, h * HEAD : (h + 1) * HEAD] = jnp.dot(
                weighted[h],
                a[:peers, (4 + h) * TOK : (5 + h) * TOK, :].reshape(width, HEAD),
                preferred_element_type=F32,
            )


def finish(b, near, far, cols, mixed_in, highest_in, inside, queries, gain, lin_out, att_out, values, att, lin, done):
    values[:, HEAD:] = jnp.ones((BLOCK, HEAD), BF16)
    values[:, :HEAD] = near[STATE_ROWS + BLOCK :, :]
    seen = (lax.broadcasted_iota(jnp.int32, (ROW_TILE, BLOCK), 1) - BLOCK).astype(F32)
    tiles = [slice(tile * ROW_TILE, (tile + 1) * ROW_TILE) for tile in range(BLOCK // ROW_TILE)]
    pieces = [slice(head * HEAD, (head + 1) * HEAD) for head in range(HEADS)]
    copies = []
    for tile, at in enumerate(tiles):
        allowed = jnp.where(seen >= cols[at, 8:9], 0.0, NEVER)
        for head, piece in enumerate(pieces):
            query = b[2 * tile : 2 * tile + 2, (4 + head) * TOK : (5 + head) * TOK, :].reshape(ROW_TILE, HEAD)
            scores = lax.dot_general(
                query,
                near[STATE_ROWS : STATE_ROWS + BLOCK, :],
                (((1,), (1,)), ((), ())),
                preferred_element_type=F32,
            )
            scores = scores * SCALE + allowed
            before = highest_in[at, piece]
            highest = jnp.maximum(jnp.max(scores, axis=1, keepdims=True), before)
            weights = [jnp.exp2(scores[:, c : c + HEAD] - highest).astype(BF16) for c in range(0, BLOCK, HEAD)]
            shrink = jnp.exp2(before - highest)
            mixed = jnp.dot(jnp.concatenate(weights, axis=1), values[...], preferred_element_type=F32)
            first = 2 * head * HEAD
            top = mixed[:, :HEAD] + shrink * mixed_in[at, first : first + HEAD]
            total = mixed[:, HEAD:] + shrink * mixed_in[at, first + HEAD : first + 2 * HEAD]
            att[at, piece] = (top / total).astype(BF16)
        copies.append(pltpu.make_async_copy(att.at[at], att_out.at[at], done.at[tile]))
        copies[-1].start()
    shrink = near[HEADS * HEAD : STATE_ROWS, :].astype(F32)
    shrink = shrink[0:8, :] + shrink[8:16, :]
    incoming = [
        (near[piece, :].astype(F32) + shrink[head : head + 1, :] * far[piece, :].astype(F32)).astype(BF16)
        for head, piece in enumerate(pieces)
    ]
    for tile, at in enumerate(tiles):
        carried = [
            jnp.dot(
                queries[head * BLOCK + tile * ROW_TILE : head * BLOCK + (tile + 1) * ROW_TILE, :],
                incoming[head],
                preferred_element_type=F32,
            )
            for head in range(HEADS)
        ]
        for head, piece in enumerate(pieces):
            combined = inside[at, piece] + carried[head] * cols[at, 4 + head : 5 + head]
            mean = jnp.mean(combined * combined, axis=1, keepdims=True)
            lin[at, piece] = (combined * lax.rsqrt(mean + 1e-6) * gain[:, piece]).astype(BF16)
        copies.append(pltpu.make_async_copy(lin.at[at], lin_out.at[at], done.at[len(tiles) + tile]))
        copies[-1].start()
    for copy in copies:
        copy.wait()


def shifted(block, distance):
    count = lax.axis_size("ctx")
    return lax.ppermute(block, "ctx", [(i, i + distance) for i in range(count - distance)])


def exchanged(packed):
    return lax.all_to_all(packed, "uly", split_axis=0, concat_axis=0, tiled=True)


def shards(q, k, v, decay, gain, lens, aq, ak, av):
    lens = lens.reshape(1, 64)
    fast = lambda dtype, *dims: pltpu.VMEM(dims, dtype)
    shape = lambda *dims: jax.ShapeDtypeStruct(dims, BF16)
    wide, narrow = PEERS * HEADS * HEAD, PEERS * HEAD
    far_core = lambda x: pltpu.with_memory_space_constraint(x, pltpu.HBM)
    in_hbm = pl.BlockSpec(memory_space=pltpu.HBM)
    first, window = call(
        pack_first,
        (shape(PEERS, ROWS_A, HEAD), shape(PEERS, 2 * TOK, HEAD)),
        [
            pltpu.VMEM((TOK, wide), BF16),
            pltpu.VMEM((TOK, wide), BF16),
            pltpu.VMEM((TOK, narrow), BF16),
            pltpu.VMEM((TOK, narrow), BF16),
            pltpu.VMEM((PEERS * HEADS, TOK), BF16),
            pltpu.VMEM((PEERS, ROWS_A, HEAD), BF16),
            pltpu.VMEM((PEERS, 2 * TOK, HEAD), BF16),
            pltpu.SemaphoreType.DMA((5,)),
            pltpu.SemaphoreType.DMA((4,)),
        ],
        [in_hbm] * 5,
        in_hbm,
    )(*(far_core(x) for x in (k, v, ak, av, decay.T)))
    a = near_core(exchanged(first))
    earlier = shifted(window, 2)
    second = call(
        pack_body, pltpu.HBM((PEERS, ROWS_B, HEAD), BF16),
        [pltpu.VMEM((PEERS, 8 * TOK, HEAD), BF16), pltpu.SemaphoreType.DMA], output=in_hbm,
    )(q, aq)
    second = pl.pallas_call(
        insert,
        out_shape=pltpu.HBM((PEERS, ROWS_B, HEAD), BF16),
        in_specs=[pl.BlockSpec(memory_space=pltpu.VMEM), in_hbm],
        out_specs=in_hbm,
        input_output_aliases={1: 0},
        scratch_shapes=[pltpu.SemaphoreType.DMA],
    )(near_core(earlier), far_core(second))
    b = near_core(exchanged(second))
    own, all_own, cols, rows = call(
        state,
        (
            fast(BF16, STATE_ROWS, HEAD),
            fast(BF16, STATE_ROWS + 2 * BLOCK, HEAD),
            fast(F32, BLOCK, HEAD),
            fast(F32, 16, BLOCK),
        ),
    )(a, lens)
    near, far = near_core(shifted(all_own, 1)), near_core(shifted(own, 2))
    cols, rows = near_core(cols), near_core(rows)
    mixed, highest, inside, queries = call(
        within,
        (
            fast(F32, BLOCK, 2 * HEADS * HEAD),
            fast(F32, BLOCK, HEADS * HEAD),
            fast(F32, BLOCK, HEADS * HEAD),
            fast(BF16, HEADS * BLOCK, HEAD),
        ),
        [
            pltpu.VMEM((2 * BLOCK, HEAD), BF16),
            pltpu.VMEM((2 * BLOCK, 2 * HEAD), BF16),
            pltpu.VMEM((ROW_TILE, PART), F32),
            pltpu.VMEM((HEADS * BLOCK, HEAD), BF16),
        ],
    )(a, b, cols, rows)
    lin_out, att_out = call(
        finish,
        (shape(BLOCK, HEADS * HEAD), shape(BLOCK, HEADS * HEAD)),
        [
            pltpu.VMEM((BLOCK, 2 * HEAD), BF16),
            pltpu.VMEM((BLOCK, HEADS * HEAD), BF16),
            pltpu.VMEM((BLOCK, HEADS * HEAD), BF16),
            pltpu.SemaphoreType.DMA((2 * BLOCK // ROW_TILE,)),
        ],
        output=in_hbm,
    )(
        b,
        near,
        far,
        cols,
        near_core(mixed),
        near_core(highest),
        near_core(inside),
        near_core(queries),
        gain.reshape(1, HEADS * HEAD),
    )
    return lin_out, att_out


def solution(mesh):
    rows = P(("ctx", "uly"), None)
    return jax.shard_map(
        shards,
        mesh=mesh,
        in_specs=(rows, rows, rows, rows, P("uly"), P(), rows, rows, rows),
        out_specs=(P("ctx", "uly"), P("ctx", "uly")),
        check_vma=False,
    )
```

time: 64.5 us -> 62.7 us (0.972)
  the two profiles are of different devices: /device:TPU:56 before, /device:TPU:58 now
where the time goes in v3:
time: 62.7 us; the launch traced here: 62.4 us
  waiting for transfers between devices  28.7 us (46%)
  starting transfers between devices  19.8 us (32%)
  Pallas kernels  13.2 us (21%)
  between operations  0.74 us (1%)
    ppermute x3, waiting for transfers between devices, shifted(): lax.ppermute(block, 'ctx', [(i, i + distance) for i in range(count - dist...  18.4 us
    all_to_all x2, waiting for transfers between devices, exchanged(): lax.all_to_all(packed, 'uly', split_axis=0, concat_axis=0, tiled=True)  10.3 us
    ppermute x3, starting transfers between devices, shifted(): lax.ppermute(block, 'ctx', [(i, i + distance) for i in range(count - dist...  10 us
    all_to_all x2, starting transfers between devices, exchanged(): lax.all_to_all(packed, 'uly', split_axis=0, concat_axis=0, tiled=True)  9.79 us
    pallas_call x1, Pallas kernels, shards(): call(within, (fast(F32, BLOCK, 2 * HEADS * HEAD), fast(F32, BLOCK, HEADS...  3.76 us
    pallas_call x1, Pallas kernels, shards(): call(finish, (shape(BLOCK, HEADS * HEAD), shape(BLOCK, HEADS * HEAD)), [p...  3.08 us
    pallas_call x1, Pallas kernels, shards(): call(pack_first, (shape(PEERS, ROWS_A, HEAD), shape(PEERS, 2 * TOK, HEAD)...  2.32 us
    pallas_call x1, Pallas kernels, shards(): call(state, (fast(BF16, STATE_ROWS, HEAD), fast(BF16, STATE_ROWS + 2 * BL...  2.12 us
  transfers between devices with their start and end apart: 5, of which 3 were waited for; matrix products, arithmetic and copies ran while one was open for 0% of the time, Pallas kernels for 12%

profile of v3, /device:TPU:58, one launch (start us, length us, event | category | flops | bytes accessed | tf_op | source)
XLA Modules:
  0.0 62.4 jit_solution(11695283737395946077)
XLA Ops:
  0.6 2.3 %shard_map.104 = (bf16[8,656,128]{2,1,0:T(8,128)(2,1)}, bf16[8,128,128]{2,1,0:T(8,128)(2,1)S(1)}) custom-call(bf16[64,4096]{1,0:T(8,128)(2,1)} %k.1, bf16[64,4096]{1,0:T(8,128)(2,1)} %v.1, bf16[64,1024]{1,0:T(8,128)(2,1)} %ak.1, bf16[64,1024]{1,0:T(8,128)(2,1)} %av.1, bf16[32,64]{1,0:T(8,128)(2,1)} %bitcast.5), custom_call_target="tpu_custom_call" | custom-call | tf_op jit(solution)/shard_map/pallas_call | solution.py:300
  3.0 0.0 copy-start
  3.0 0.0 copy-start.1
  3.0 5.0 %all-to-all-start.1 = ((bf16[8,656,128]{2,1,0:T(8,128)(2,1)}), bf16[8,656,128]{2,1,0:T(8,128)(2,1)S(1)}, u32[]{:S(2)}, u32[]{:S(2)}) async-start(bf16[8,656,128]{2,1,0:T(8,128)(2,1)} %get-tuple-element.13), calls=%async_computation.1 | async-start | bytes 2686976 | tf_op jit(solution)/shard_map/all_to_all | solution.py:290
  8.0 5.2 %collective-permute-start = (bf16[8,128,128]{2,1,0:T(8,128)(2,1)S(1)}, bf16[8,128,128]{2,1,0:T(8,128)(2,1)S(1)}, u32[]{:S(2)}, u32[]{:S(2)}) collective-permute-start(bf16[8,128,128]{2,1,0:T(8,128)(2,1)S(1)} %get-tuple-element.12), channel_id=1, source_target_pairs={{0,16},{8,24},{16,32},{24,40},{32,48},{40,56},{48,64},{56,72},{64,... | collective-permute-start | bytes 786440 | tf_op jit(solution)/shard_map/ppermute | solution.py:286
  13.1 0.0 copy-done
  13.1 0.0 copy-done.1
  13.2 1.2 %shard_map.105.packed = bf16[8,640,128]{2,1,0:T(8,128)(2,1)} custom-call(bf16[64,4096]{1,0:T(8,128)(2,1)S(1)} %copy-done, bf16[64,4096]{1,0:T(8,128)(2,1)S(1)} %copy-done.1), custom_call_target="tpu_custom_call" | custom-call | tf_op jit(solution)/shard_map/pallas_call | solution.py:319
  14.3 17.0 %collective-permute-done.earlier = bf16[8,128,128]{2,1,0:T(8,128)(2,1)S(1)} collective-permute-done((bf16[8,128,128]{2,1,0:T(8,128)(2,1)S(1)}, bf16[8,128,128]{2,1,0:T(8,128)(2,1)S(1)}, u32[]{:S(2)}, u32[]{:S(2)}) %collective-permute-start) | collective-permute-done | bytes 262176 | tf_op jit(solution)/shard_map/ppermute | solution.py:286
  31.3 0.7 %shard_map.106 = bf16[8,640,128]{2,1,0:T(8,128)(2,1)} custom-call(bf16[8,128,128]{2,1,0:T(8,128)(2,1)S(1)} %collective-permute-done.earlier, bf16[8,640,128]{2,1,0:T(8,128)(2,1)} %shard_map.105.packed), custom_call_target="tpu_custom_call", output_to_operand_aliasing={{}: (1, {})} | custom-call | tf_op jit(solution)/shard_map/pallas_call | solution.py:323
  32.0 0.0 copy-start.3
  32.0 0.0 all-to-all-done.1.a
  32.0 4.8 %all-to-all-start = ((bf16[8,640,128]{2,1,0:T(8,128)(2,1)}), bf16[8,640,128]{2,1,0:T(8,128)(2,1)S(1)}, u32[]{:S(2)}, u32[]{:S(2)}) async-start(bf16[8,640,128]{2,1,0:T(8,128)(2,1)} %shard_map.106), calls=%async_computation | async-start | bytes 2621440 | tf_op jit(solution)/shard_map/all_to_all | solution.py:290
  36.9 0.0 copy-done.3
  36.9 2.1 %shard_map.107 = (bf16[528,128]{1,0:T(8,128)(2,1)}, bf16[1552,128]{1,0:T(8,128)(2,1)}, f32[512,128]{1,0:T(8,128)S(1)}, f32[16,512]{1,0:T(8,128)S(1)}) custom-call(bf16[8,656,128]{2,1,0:T(8,128)(2,1)S(1)} %all-to-all-done.1.a, s32[1,64]{1,0:T(1,128)S(1)} %bitcast.4), custom_call_target="tpu_custom_call" | custom-call | tf_op jit(solution)/shard_map/pallas_call | solution.py:332
  39.0 1.9 %collective-permute-start.1 = (bf16[1552,128]{1,0:T(8,128)(2,1)}, bf16[1552,128]{1,0:T(8,128)(2,1)S(1)}, u32[]{:S(2)}, u32[]{:S(2)}) collective-permute-start(bf16[1552,128]{1,0:T(8,128)(2,1)} %get-tuple-element.14), channel_id=1, source_target_pairs={{0,8},{8,16},{16,24},{24,32},{32,40},{40,48},{48,56},{56,64},{64,7... | collective-permute-start | bytes 1191944 | tf_op jit(solution)/shard_map/ppermute | solution.py:286
  40.9 3.0 %collective-permute-start.2 = (bf16[528,128]{1,0:T(8,128)(2,1)}, bf16[528,128]{1,0:T(8,128)(2,1)S(1)}, u32[]{:S(2)}, u32[]{:S(2)}) collective-permute-start(bf16[528,128]{1,0:T(8,128)(2,1)} %get-tuple-element.15), channel_id=1, source_target_pairs={{0,16},{8,24},{16,32},{24,40},{32,48},{40,56},{48,64},{56,72},{64,... | collective-permute-start | bytes 405512 | tf_op jit(solution)/shard_map/ppermute | solution.py:286
  43.9 10.3 %all-to-all-done.b = bf16[8,640,128]{2,1,0:T(8,128)(2,1)S(1)} async-done(((bf16[8,640,128]{2,1,0:T(8,128)(2,1)}), bf16[8,640,128]{2,1,0:T(8,128)(2,1)S(1)}, u32[]{:S(2)}, u32[]{:S(2)}) %all-to-all-start) | async-done | bytes 1310752 | tf_op jit(solution)/shard_map/all_to_all | solution.py:290
  54.2 0.0 copy-start.2
  54.2 3.8 %shard_map.108 = (f32[512,1024]{1,0:T(8,128)S(1)}, f32[512,512]{1,0:T(8,128)S(1)}, f32[512,512]{1,0:T(8,128)S(1)}, bf16[2048,128]{1,0:T(8,128)(2,1)S(1)}) custom-call(bf16[8,656,128]{2,1,0:T(8,128)(2,1)S(1)} %all-to-all-done.1.a, bf16[8,640,128]{2,1,0:T(8,128)(2,1)S(1)} %all-to-all-done.b, f32[512,128]{1,0:T(8,128)S(1)} %get-tuple-element.16.cols, ...), custom_call_target="tpu_custom_call" | custom-call | tf_op jit(solution)/shard_map/pallas_call | solution.py:343
  57.9 1.4 %collective-permute-done.2.far = bf16[528,128]{1,0:T(8,128)(2,1)S(1)} collective-permute-done((bf16[528,128]{1,0:T(8,128)(2,1)}, bf16[528,128]{1,0:T(8,128)(2,1)S(1)}, u32[]{:S(2)}, u32[]{:S(2)}) %collective-permute-start.2) | collective-permute-done | bytes 135200 | tf_op jit(solution)/shard_map/ppermute | solution.py:286
  59.3 0.0 collective-permute-done.1.near
  59.3 0.0 copy-done.2
  59.3 3.1 %shard_map.109 = (bf16[512,512]{1,0:T(8,128)(2,1)}, bf16[512,512]{1,0:T(8,128)(2,1)}) custom-call(bf16[8,640,128]{2,1,0:T(8,128)(2,1)S(1)} %all-to-all-done.b, bf16[1552,128]{1,0:T(8,128)(2,1)S(1)} %collective-permute-done.1.near, bf16[528,128]{1,0:T(8,128)(2,1)S(1)} %collective-permute-done.2.far, f32[512,128]{1,0:T(8,128)S(1)} %get-tuple-element.16.cols, ...), custom_call_target="tpu_custom_call" | custom-call | tf_op jit(solution)/shard_map/pallas_call | solution.py:358
Async XLA Ops:
  3.0 10.2 %copy-start = (bf16[64,4096]{1,0:T(8,128)(2,1)S(1)}, bf16[64,4096]{1,0:T(8,128)(2,1)}, u32[]{:S(2)}) copy-start(bf16[64,4096]{1,0:T(8,128)(2,1)} %q.1) | copy-start | bytes 1572868
  3.0 10.2 %copy-start.1 = (bf16[64,4096]{1,0:T(8,128)(2,1)S(1)}, bf16[64,4096]{1,0:T(8,128)(2,1)}, u32[]{:S(2)}) copy-start(bf16[64,4096]{1,0:T(8,128)(2,1)} %aq.1) | copy-start | bytes 1572868
  3.0 29.0 %all-to-all-start.1 = ((bf16[8,656,128]{2,1,0:T(8,128)(2,1)}), bf16[8,656,128]{2,1,0:T(8,128)(2,1)S(1)}, u32[]{:S(2)}, u32[]{:S(2)}) async-start(bf16[8,656,128]{2,1,0:T(8,128)(2,1)} %get-tuple-element.13), calls=%async_computation.1 | async-start | bytes 2686976 | tf_op jit(solution)/shard_map/all_to_all | solution.py:290
  8.0 23.3 %collective-permute-start = (bf16[8,128,128]{2,1,0:T(8,128)(2,1)S(1)}, bf16[8,128,128]{2,1,0:T(8,128)(2,1)S(1)}, u32[]{:S(2)}, u32[]{:S(2)}) collective-permute-start(bf16[8,128,128]{2,1,0:T(8,128)(2,1)S(1)} %get-tuple-element.12), channel_id=1, source_target_pairs={{0,16},{8,24},{16,32},{24,40},{32,48},{40,56},{48,64},{56,72},{64,... | collective-permute-start | bytes 786440 | tf_op jit(solution)/shard_map/ppermute | solution.py:286
  32.0 4.8 %copy-start.3 = (s32[64]{0:T(128)S(1)}, s32[64]{0:T(128)}, u32[]{:S(2)}) copy-start(s32[64]{0:T(128)} %param.14) | copy-start | bytes 772
  32.0 22.1 %all-to-all-start = ((bf16[8,640,128]{2,1,0:T(8,128)(2,1)}), bf16[8,640,128]{2,1,0:T(8,128)(2,1)S(1)}, u32[]{:S(2)}, u32[]{:S(2)}) async-start(bf16[8,640,128]{2,1,0:T(8,128)(2,1)} %shard_map.106), calls=%async_computation | async-start | bytes 2621440 | tf_op jit(solution)/shard_map/all_to_all | solution.py:290
  39.0 20.3 %collective-permute-start.1 = (bf16[1552,128]{1,0:T(8,128)(2,1)}, bf16[1552,128]{1,0:T(8,128)(2,1)S(1)}, u32[]{:S(2)}, u32[]{:S(2)}) collective-permute-start(bf16[1552,128]{1,0:T(8,128)(2,1)} %get-tuple-element.14), channel_id=1, source_target_pairs={{0,8},{8,16},{16,24},{24,32},{32,40},{40,48},{48,56},{56,64},{64,7... | collective-permute-start | bytes 1191944 | tf_op jit(solution)/shard_map/ppermute | solution.py:286
  40.9 18.4 %collective-permute-start.2 = (bf16[528,128]{1,0:T(8,128)(2,1)}, bf16[528,128]{1,0:T(8,128)(2,1)S(1)}, u32[]{:S(2)}, u32[]{:S(2)}) collective-permute-start(bf16[528,128]{1,0:T(8,128)(2,1)} %get-tuple-element.15), channel_id=1, source_target_pairs={{0,16},{8,24},{16,32},{24,40},{32,48},{40,56},{48,64},{56,72},{64,... | collective-permute-start | bytes 405512 | tf_op jit(solution)/shard_map/ppermute | solution.py:286
  54.2 5.2 %copy-start.2 = (f32[512]{0:T(512)S(1)}, f32[512]{0:T(512)}, u32[]{:S(2)}) copy-start(f32[512]{0:T(512)} %param.13) | copy-start | bytes 6148

commit v4 on v3

--- a/solution.py
+++ b/solution.py
@@ -106,7 +106,7 @@
     copy.wait()
 
 
-def begins(lens):
+def starts(lens):
     start = lax.axis_index("ctx") * BLOCK
     lane = lax.broadcasted_iota(jnp.int32, (8, 128), 1)
     row = jnp.concatenate([lens[...], jnp.zeros((1, 64), jnp.int32)], axis=1)
@@ -115,9 +115,7 @@
     for step in (1, 2, 4, 8, 16, 32):
         total = total + jnp.where(lane >= step, pltpu.roll(total, step, 1), 0)
     first = (total - row)[0:1, :] - start
-    first = jnp.where(lane[0:1, :] < 64, first, 1 << 20).astype(F32)
-    place = lax.broadcasted_iota(jnp.int32, (BLOCK, 128), 0).astype(F32)
-    return jnp.max(jnp.where(first <= place, first, -float(1 << 20)), axis=1, keepdims=True)
+    return jnp.where(lane[0:1, :] < 64, first, 1 << 20).astype(F32)
 
 
 def decay_rows(a):
@@ -140,36 +138,37 @@
     return a[:, index * TOK : (index + 1) * TOK, :].reshape(BLOCK, HEAD)
 
 
-def state(a, lens, out, all_out, cols, rows):
+def state(a, lens, out):
+    first = starts(lens)
+    last = jnp.max(jnp.where(first <= float(BLOCK - 1), first, -float(1 << 20)), axis=1, keepdims=True)
+    sums = decay_rows(a)
+    end = sums[:, BLOCK - 1 : BLOCK]
+    place = lax.broadcasted_iota(jnp.int32, (16, BLOCK), 1).astype(F32)
+    weight = jnp.exp2(jnp.where(place >= last, sums - end, NEVER))
+    weight = jnp.transpose(jnp.concatenate([weight, jnp.zeros((112, BLOCK), F32)], axis=0))
+    for head in range(HEADS):
+        end_keys = (silu(gathered(a, head)).astype(F32) * weight[:, head : head + 1]).astype(BF16)
+        total = lax.dot_general(
+            end_keys, gathered(a, 4 + head), (((0,), (0,)), ((), ())), preferred_element_type=F32
+        )
+        out[head * HEAD : (head + 1) * HEAD, :] = total.astype(BF16)
+    decay = jnp.broadcast_to(jnp.where(last < 0, jnp.exp2(-end[0:8, :]), 0.0), (8, HEAD))
+    high = decay.astype(BF16).astype(F32)
+    out[HEADS * HEAD :, :] = jnp.concatenate([high, decay - high], axis=0).astype(BF16)
+
+
+def prepare(a, lens, cols, rows, kv):
     for index in range(2):
-        all_out[STATE_ROWS + index * BLOCK : STATE_ROWS + (index + 1) * BLOCK, :] = gathered(a, 8 + index)
-    begin = begins(lens)
+        kv[index * BLOCK : (index + 1) * BLOCK, :] = gathered(a, 8 + index)
+    first = starts(lens)
+    place = lax.broadcasted_iota(jnp.int32, (BLOCK, 128), 0).astype(F32)
+    begin = jnp.max(jnp.where(first <= place, first, -float(1 << 20)), axis=1, keepdims=True)
     sums = decay_rows(a)
     rows[...] = sums
     turned = jnp.transpose(jnp.concatenate([sums, jnp.zeros((112, BLOCK), F32)], axis=0))
     lane = lax.broadcasted_iota(jnp.int32, (BLOCK, HEAD), 1)
     carry = jnp.where(begin < 0, jnp.exp2(-turned), 0.0)
     cols[...] = jnp.where(lane < HEADS, turned, jnp.where(lane == 8, begin, carry))
-    last = begin[BLOCK - 1 : BLOCK, :]
-    end = turned[BLOCK - 1 : BLOCK, :]
-    place = lax.broadcasted_iota(jnp.int32, (BLOCK, 1), 0).astype(F32)
-    weight = jnp.exp2(jnp.where(place >= last, turned - end, NEVER))
-    extra = []
-    for head in range(HEADS):
-        key_map = silu(gathered(a, head))
-        end_keys = (key_map.astype(F32) * weight[:, head : head + 1]).astype(BF16)
-        total = lax.dot_general(
-            end_keys, gathered(a, 4 + head), (((0,), (0,)), ((), ())), preferred_element_type=F32
-        )
-        out[head * HEAD : (head + 1) * HEAD, :] = total.astype(BF16)
-        all_out[head * HEAD : (head + 1) * HEAD, :] = total.astype(BF16)
-        gone = jnp.where(last < 0, jnp.exp2(-end[:, head : head + 1]), 0.0)
-        extra.append(jnp.broadcast_to(gone, (1, HEAD)))
-    decay = jnp.concatenate([*extra, jnp.zeros((4, HEAD), F32)], axis=0)
-    high = decay.astype(BF16).astype(F32)
-    parts = jnp.concatenate([high, decay - high], axis=0).astype(BF16)
-    out[HEADS * HEAD :, :] = parts
-    all_out[HEADS * HEAD : STATE_ROWS, :] = parts
 
 
 def within(a, b, cols, rows, mixed_out, highest_out, inside_out, queries, keys, values, bias, maps):
@@ -227,9 +226,9 @@
             )
 
 
-def finish(b, near, far, cols, mixed_in, highest_in, inside, queries, gain, lin_out, att_out, values, att, lin, done):
+def finish(b, kv1, near, far, cols, mixed_in, highest_in, inside, queries, gain, lin_out, att_out, values, att, lin, done):
     values[:, HEAD:] = jnp.ones((BLOCK, HEAD), BF16)
-    values[:, :HEAD] = near[STATE_ROWS + BLOCK :, :]
+    values[:, :HEAD] = kv1[BLOCK:, :]
     seen = (lax.broadcasted_iota(jnp.int32, (ROW_TILE, BLOCK), 1) - BLOCK).astype(F32)
     tiles = [slice(tile * ROW_TILE, (tile + 1) * ROW_TILE) for tile in range(BLOCK // ROW_TILE)]
     pieces = [slice(head * HEAD, (head + 1) * HEAD) for head in range(HEADS)]
@@ -240,7 +239,7 @@
             query = b[2 * tile : 2 * tile + 2, (4 + head) * TOK : (5 + head) * TOK, :].reshape(ROW_TILE, HEAD)
             scores = lax.dot_general(
                 query,
-                near[STATE_ROWS : STATE_ROWS + BLOCK, :],
+                kv1[:BLOCK, :],
                 (((1,), (1,)), ((), ())),
                 preferred_element_type=F32,
             )
@@ -329,16 +328,12 @@
         scratch_shapes=[pltpu.SemaphoreType.DMA],
     )(near_core(earlier), far_core(second))
     b = near_core(exchanged(second))
-    own, all_own, cols, rows = call(
-        state,
-        (
-            fast(BF16, STATE_ROWS, HEAD),
-            fast(BF16, STATE_ROWS + 2 * BLOCK, HEAD),
-            fast(F32, BLOCK, HEAD),
-            fast(F32, 16, BLOCK),
-        ),
+    own = call(state, fast(BF16, STATE_ROWS, HEAD))(a, lens)
+    far, near = near_core(shifted(own, 2)), near_core(shifted(own, 1))
+    cols, rows, kv = call(
+        prepare, (fast(F32, BLOCK, HEAD), fast(F32, 16, BLOCK), fast(BF16, 2 * BLOCK, HEAD))
     )(a, lens)
-    near, far = near_core(shifted(all_own, 1)), near_core(shifted(own, 2))
+    kv1 = near_core(shifted(kv, 1))
     cols, rows = near_core(cols), near_core(rows)
     mixed, highest, inside, queries = call(
         within,
@@ -367,6 +362,7 @@
         output=in_hbm,
     )(
         b,
+        kv1,
         near,
         far,
         cols,

time: 62.7 us -> 62.4 us (level)
  the two profiles are of different devices: /device:TPU:58 before, /device:TPU:56 now
where the time goes in v4:
time: 62.4 us; the launch traced here: 62.1 us
  waiting for transfers between devices  25 us (40%)
  starting transfers between devices  21.8 us (35%)
  Pallas kernels  14.4 us (23%)
  between operations  0.78 us (1%)
    ppermute x4, waiting for transfers between devices, shifted(): lax.ppermute(block, 'ctx', [(i, i + distance) for i in range(count - dist...  17.3 us
    ppermute x4, starting transfers between devices, shifted(): lax.ppermute(block, 'ctx', [(i, i + distance) for i in range(count - dist...  12.9 us
    all_to_all x2, starting transfers between devices, exchanged(): lax.all_to_all(packed, 'uly', split_axis=0, concat_axis=0, tiled=True)  8.9 us
    all_to_all x2, waiting for transfers between devices, exchanged(): lax.all_to_all(packed, 'uly', split_axis=0, concat_axis=0, tiled=True)  7.71 us
    pallas_call x1, Pallas kernels, shards(): call(within, (fast(F32, BLOCK, 2 * HEADS * HEAD), fast(F32, BLOCK, HEADS...  3.77 us
    pallas_call x1, Pallas kernels, shards(): call(finish, (shape(BLOCK, HEADS * HEAD), shape(BLOCK, HEADS * HEAD)), [p...  3.1 us
    pallas_call x1, Pallas kernels, shards(): call(pack_first, (shape(PEERS, ROWS_A, HEAD), shape(PEERS, 2 * TOK, HEAD)...  2.35 us
    pallas_call x1, Pallas kernels, shards(): own = call(state, fast(BF16, STATE_ROWS, HEAD))(a, lens)  1.97 us
  transfers between devices with their start and end apart: 6, of which 2 were waited for; matrix products, arithmetic and copies ran while one was open for 0% of the time, Pallas kernels for 14%

profile of v4, /device:TPU:56, one launch (start us, length us, event | category | flops | bytes accessed | tf_op | source)
XLA Modules:
  0.0 62.1 jit_solution(16696275313998251111)
XLA Ops:
  0.6 2.3 %shard_map.104 = (bf16[8,656,128]{2,1,0:T(8,128)(2,1)}, bf16[8,128,128]{2,1,0:T(8,128)(2,1)S(1)}) custom-call(bf16[64,4096]{1,0:T(8,128)(2,1)} %k.1, bf16[64,4096]{1,0:T(8,128)(2,1)} %v.1, bf16[64,1024]{1,0:T(8,128)(2,1)} %ak.1, bf16[64,1024]{1,0:T(8,128)(2,1)} %av.1, bf16[32,64]{1,0:T(8,128)(2,1)} %bitcast.6), custom_call_target="tpu_custom_call" | custom-call | tf_op jit(solution)/shard_map/pallas_call | solution.py:299
  3.0 0.0 copy-start
  3.0 0.0 copy-start.1
  3.0 4.4 %all-to-all-start.1 = ((bf16[8,656,128]{2,1,0:T(8,128)(2,1)}), bf16[8,656,128]{2,1,0:T(8,128)(2,1)S(1)}, u32[]{:S(2)}, u32[]{:S(2)}) async-start(bf16[8,656,128]{2,1,0:T(8,128)(2,1)} %get-tuple-element.12), calls=%async_computation.1 | async-start | bytes 2686976 | tf_op jit(solution)/shard_map/all_to_all | solution.py:289
  7.5 5.2 %collective-permute-start = (bf16[8,128,128]{2,1,0:T(8,128)(2,1)S(1)}, bf16[8,128,128]{2,1,0:T(8,128)(2,1)S(1)}, u32[]{:S(2)}, u32[]{:S(2)}) collective-permute-start(bf16[8,128,128]{2,1,0:T(8,128)(2,1)S(1)} %get-tuple-element.11), channel_id=1, source_target_pairs={{0,16},{8,24},{16,32},{24,40},{32,48},{40,56},{48,64},{56,72},{64,... | collective-permute-start | bytes 786440 | tf_op jit(solution)/shard_map/ppermute | solution.py:285
  12.6 0.0 copy-done
  12.6 1.2 %shard_map.105.packed = bf16[8,640,128]{2,1,0:T(8,128)(2,1)} custom-call(bf16[64,4096]{1,0:T(8,128)(2,1)S(1)} %copy-done, bf16[64,4096]{1,0:T(8,128)(2,1)S(1)} %copy-done.1), custom_call_target="tpu_custom_call" | custom-call | tf_op jit(solution)/shard_map/pallas_call | solution.py:318
  13.8 17.3 %collective-permute-done.earlier = bf16[8,128,128]{2,1,0:T(8,128)(2,1)S(1)} collective-permute-done((bf16[8,128,128]{2,1,0:T(8,128)(2,1)S(1)}, bf16[8,128,128]{2,1,0:T(8,128)(2,1)S(1)}, u32[]{:S(2)}, u32[]{:S(2)}) %collective-permute-start) | collective-permute-done | bytes 262176 | tf_op jit(solution)/shard_map/ppermute | solution.py:285
  31.2 0.8 %shard_map.106 = bf16[8,640,128]{2,1,0:T(8,128)(2,1)} custom-call(bf16[8,128,128]{2,1,0:T(8,128)(2,1)S(1)} %collective-permute-done.earlier, bf16[8,640,128]{2,1,0:T(8,128)(2,1)} %shard_map.105.packed), custom_call_target="tpu_custom_call", output_to_operand_aliasing={{}: (1, {})} | custom-call | tf_op jit(solution)/shard_map/pallas_call | solution.py:322
  31.9 0.0 copy-start.3
  31.9 0.0 all-to-all-done.1.a
  31.9 4.5 %all-to-all-start = ((bf16[8,640,128]{2,1,0:T(8,128)(2,1)}), bf16[8,640,128]{2,1,0:T(8,128)(2,1)S(1)}, u32[]{:S(2)}, u32[]{:S(2)}) async-start(bf16[8,640,128]{2,1,0:T(8,128)(2,1)} %shard_map.106), calls=%async_computation | async-start | bytes 2621440 | tf_op jit(solution)/shard_map/all_to_all | solution.py:289
  36.4 1.3 %shard_map.107 = (f32[512,128]{1,0:T(8,128)S(1)}, f32[16,512]{1,0:T(8,128)S(1)}, bf16[1024,128]{1,0:T(8,128)(2,1)}) custom-call(bf16[8,656,128]{2,1,0:T(8,128)(2,1)S(1)} %all-to-all-done.1.a, s32[1,64]{1,0:T(1,128)S(1)} %bitcast.4), custom_call_target="tpu_custom_call" | custom-call | tf_op jit(solution)/shard_map/pallas_call | solution.py:333
  37.7 1.9 %collective-permute-start.1 = (bf16[1024,128]{1,0:T(8,128)(2,1)}, bf16[1024,128]{1,0:T(8,128)(2,1)S(1)}, u32[]{:S(2)}, u32[]{:S(2)}) collective-permute-start(bf16[1024,128]{1,0:T(8,128)(2,1)} %get-tuple-element.13), channel_id=1, source_target_pairs={{0,8},{8,16},{16,24},{24,32},{32,40},{40,48},{48,56},{56,64},{64,7... | collective-permute-start | bytes 786440 | tf_op jit(solution)/shard_map/ppermute | solution.py:285
  39.6 2.0 %shard_map.108 = bf16[528,128]{1,0:T(8,128)(2,1)} custom-call(bf16[8,656,128]{2,1,0:T(8,128)(2,1)S(1)} %all-to-all-done.1.a, s32[1,64]{1,0:T(1,128)S(1)} %bitcast.5), custom_call_target="tpu_custom_call" | custom-call | tf_op jit(solution)/shard_map/pallas_call | solution.py:331
  41.6 1.9 %collective-permute-start.2 = (bf16[528,128]{1,0:T(8,128)(2,1)}, bf16[528,128]{1,0:T(8,128)(2,1)S(1)}, u32[]{:S(2)}, u32[]{:S(2)}) collective-permute-start(bf16[528,128]{1,0:T(8,128)(2,1)} %shard_map.108), channel_id=1, source_target_pairs={{0,8},{8,16},{16,24},{24,32},{32,40},{40,48},{48,56},{56,64},{64,7... | collective-permute-start | bytes 405512 | tf_op jit(solution)/shard_map/ppermute | solution.py:285
  43.5 4.0 %collective-permute-start.3 = (bf16[528,128]{1,0:T(8,128)(2,1)}, bf16[528,128]{1,0:T(8,128)(2,1)S(1)}, u32[]{:S(2)}, u32[]{:S(2)}) collective-permute-start(bf16[528,128]{1,0:T(8,128)(2,1)} %shard_map.108), channel_id=1, source_target_pairs={{0,16},{8,24},{16,32},{24,40},{32,48},{40,56},{48,64},{56,72},{64,... | collective-permute-start | bytes 405512 | tf_op jit(solution)/shard_map/ppermute | solution.py:285
  47.5 7.7 %all-to-all-done.b = bf16[8,640,128]{2,1,0:T(8,128)(2,1)S(1)} async-done(((bf16[8,640,128]{2,1,0:T(8,128)(2,1)}), bf16[8,640,128]{2,1,0:T(8,128)(2,1)S(1)}, u32[]{:S(2)}, u32[]{:S(2)}) %all-to-all-start) | async-done | bytes 1310752 | tf_op jit(solution)/shard_map/all_to_all | solution.py:289
  55.2 3.8 %shard_map.109 = (f32[512,1024]{1,0:T(8,128)S(1)}, f32[512,512]{1,0:T(8,128)S(1)}, f32[512,512]{1,0:T(8,128)S(1)}, bf16[2048,128]{1,0:T(8,128)(2,1)S(1)}) custom-call(bf16[8,656,128]{2,1,0:T(8,128)(2,1)S(1)} %all-to-all-done.1.a, bf16[8,640,128]{2,1,0:T(8,128)(2,1)S(1)} %all-to-all-done.b, f32[512,128]{1,0:T(8,128)S(1)} %get-tuple-element.14.cols, ...), custom_call_target="tpu_custom_call" | custom-call | tf_op jit(solution)/shard_map/pallas_call | solution.py:338
  58.9 0.0 collective-permute-done.2.near
  59.0 0.0 collective-permute-done.3.far
  59.0 0.0 collective-permute-done.1.kv1
  59.0 0.0 copy-done.2
  59.0 3.1 %shard_map.110 = (bf16[512,512]{1,0:T(8,128)(2,1)}, bf16[512,512]{1,0:T(8,128)(2,1)}) custom-call(bf16[8,640,128]{2,1,0:T(8,128)(2,1)S(1)} %all-to-all-done.b, bf16[1024,128]{1,0:T(8,128)(2,1)S(1)} %collective-permute-done.1.kv1, bf16[528,128]{1,0:T(8,128)(2,1)S(1)} %collective-permute-done.2.near, bf16[528,128]{1,0:T(8,128)(2,1)S(1)} %collective-permute-done.3.far, ...), custom_call_target="tpu_custom_call" | custom-call | tf_op jit(solution)/shard_map/pallas_call | solution.py:353
  (3 shorter events, 0.0 us)
Async XLA Ops:
  3.0 9.6 %copy-start = (bf16[64,4096]{1,0:T(8,128)(2,1)S(1)}, bf16[64,4096]{1,0:T(8,128)(2,1)}, u32[]{:S(2)}) copy-start(bf16[64,4096]{1,0:T(8,128)(2,1)} %q.1) | copy-start | bytes 1572868
  3.0 9.6 %copy-start.1 = (bf16[64,4096]{1,0:T(8,128)(2,1)S(1)}, bf16[64,4096]{1,0:T(8,128)(2,1)}, u32[]{:S(2)}) copy-start(bf16[64,4096]{1,0:T(8,128)(2,1)} %aq.1) | copy-start | bytes 1572868
  3.0 28.9 %all-to-all-start.1 = ((bf16[8,656,128]{2,1,0:T(8,128)(2,1)}), bf16[8,656,128]{2,1,0:T(8,128)(2,1)S(1)}, u32[]{:S(2)}, u32[]{:S(2)}) async-start(bf16[8,656,128]{2,1,0:T(8,128)(2,1)} %get-tuple-element.12), calls=%async_computation.1 | async-start | bytes 2686976 | tf_op jit(solution)/shard_map/all_to_all | solution.py:289
  7.5 23.7 %collective-permute-start = (bf16[8,128,128]{2,1,0:T(8,128)(2,1)S(1)}, bf16[8,128,128]{2,1,0:T(8,128)(2,1)S(1)}, u32[]{:S(2)}, u32[]{:S(2)}) collective-permute-start(bf16[8,128,128]{2,1,0:T(8,128)(2,1)S(1)} %get-tuple-element.11), channel_id=1, source_target_pairs={{0,16},{8,24},{16,32},{24,40},{32,48},{40,56},{48,64},{56,72},{64,... | collective-permute-start | bytes 786440 | tf_op jit(solution)/shard_map/ppermute | solution.py:285
  31.9 4.5 %copy-start.3 = (s32[64]{0:T(128)S(1)}, s32[64]{0:T(128)}, u32[]{:S(2)}) copy-start(s32[64]{0:T(128)} %param.14) | copy-start | bytes 772
  31.9 23.2 %all-to-all-start = ((bf16[8,640,128]{2,1,0:T(8,128)(2,1)}), bf16[8,640,128]{2,1,0:T(8,128)(2,1)S(1)}, u32[]{:S(2)}, u32[]{:S(2)}) async-start(bf16[8,640,128]{2,1,0:T(8,128)(2,1)} %shard_map.106), calls=%async_computation | async-start | bytes 2621440 | tf_op jit(solution)/shard_map/all_to_all | solution.py:289
  37.7 21.3 %collective-permute-start.1 = (bf16[1024,128]{1,0:T(8,128)(2,1)}, bf16[1024,128]{1,0:T(8,128)(2,1)S(1)}, u32[]{:S(2)}, u32[]{:S(2)}) collective-permute-start(bf16[1024,128]{1,0:T(8,128)(2,1)} %get-tuple-element.13), channel_id=1, source_target_pairs={{0,8},{8,16},{16,24},{24,32},{32,40},{40,48},{48,56},{56,64},{64,7... | collective-permute-start | bytes 786440 | tf_op jit(solution)/shard_map/ppermute | solution.py:285
  41.6 17.4 %collective-permute-start.2 = (bf16[528,128]{1,0:T(8,128)(2,1)}, bf16[528,128]{1,0:T(8,128)(2,1)S(1)}, u32[]{:S(2)}, u32[]{:S(2)}) collective-permute-start(bf16[528,128]{1,0:T(8,128)(2,1)} %shard_map.108), channel_id=1, source_target_pairs={{0,8},{8,16},{16,24},{24,32},{32,40},{40,48},{48,56},{56,64},{64,7... | collective-permute-start | bytes 405512 | tf_op jit(solution)/shard_map/ppermute | solution.py:285
  43.5 15.5 %collective-permute-start.3 = (bf16[528,128]{1,0:T(8,128)(2,1)}, bf16[528,128]{1,0:T(8,128)(2,1)S(1)}, u32[]{:S(2)}, u32[]{:S(2)}) collective-permute-start(bf16[528,128]{1,0:T(8,128)(2,1)} %shard_map.108), channel_id=1, source_target_pairs={{0,16},{8,24},{16,32},{24,40},{32,48},{40,56},{48,64},{56,72},{64,... | collective-permute-start | bytes 405512 | tf_op jit(solution)/shard_map/ppermute | solution.py:285
  55.2 3.8 %copy-start.2 = (f32[512]{0:T(512)S(1)}, f32[512]{0:T(512)}, u32[]{:S(2)}) copy-start(f32[512]{0:T(512)} %param.13) | copy-start | bytes 6148

commit v5 on v3

--- a/solution.py
+++ b/solution.py
@@ -140,9 +140,7 @@
     return a[:, index * TOK : (index + 1) * TOK, :].reshape(BLOCK, HEAD)
 
 
-def state(a, lens, out, all_out, cols, rows):
-    for index in range(2):
-        all_out[STATE_ROWS + index * BLOCK : STATE_ROWS + (index + 1) * BLOCK, :] = gathered(a, 8 + index)
+def state(a, lens, out, cols, rows):
     begin = begins(lens)
     sums = decay_rows(a)
     rows[...] = sums
@@ -162,14 +160,11 @@
             end_keys, gathered(a, 4 + head), (((0,), (0,)), ((), ())), preferred_element_type=F32
         )
         out[head * HEAD : (head + 1) * HEAD, :] = total.astype(BF16)
-        all_out[head * HEAD : (head + 1) * HEAD, :] = total.astype(BF16)
         gone = jnp.where(last < 0, jnp.exp2(-end[:, head : head + 1]), 0.0)
         extra.append(jnp.broadcast_to(gone, (1, HEAD)))
     decay = jnp.concatenate([*extra, jnp.zeros((4, HEAD), F32)], axis=0)
     high = decay.astype(BF16).astype(F32)
-    parts = jnp.concatenate([high, decay - high], axis=0).astype(BF16)
-    out[HEADS * HEAD :, :] = parts
-    all_out[HEADS * HEAD : STATE_ROWS, :] = parts
+    out[HEADS * HEAD :, :] = jnp.concatenate([high, decay - high], axis=0).astype(BF16)
 
 
 def within(a, b, cols, rows, mixed_out, highest_out, inside_out, queries, keys, values, bias, maps):
@@ -227,9 +222,10 @@
             )
 
 
-def finish(b, near, far, cols, mixed_in, highest_in, inside, queries, gain, lin_out, att_out, values, att, lin, done):
+def finish(b, kv1, near, far, cols, mixed_in, highest_in, inside, queries, gain, lin_out, att_out, keys, values, att, lin, done):
     values[:, HEAD:] = jnp.ones((BLOCK, HEAD), BF16)
-    values[:, :HEAD] = near[STATE_ROWS + BLOCK :, :]
+    keys[...] = gathered(kv1, 0)
+    values[:, :HEAD] = gathered(kv1, 1)
     seen = (lax.broadcasted_iota(jnp.int32, (ROW_TILE, BLOCK), 1) - BLOCK).astype(F32)
     tiles = [slice(tile * ROW_TILE, (tile + 1) * ROW_TILE) for tile in range(BLOCK // ROW_TILE)]
     pieces = [slice(head * HEAD, (head + 1) * HEAD) for head in range(HEADS)]
@@ -240,7 +236,7 @@
             query = b[2 * tile : 2 * tile + 2, (4 + head) * TOK : (5 + head) * TOK, :].reshape(ROW_TILE, HEAD)
             scores = lax.dot_general(
                 query,
-                near[STATE_ROWS : STATE_ROWS + BLOCK, :],
+                keys[...],
                 (((1,), (1,)), ((), ())),
                 preferred_element_type=F32,
             )
@@ -314,7 +310,10 @@
         [in_hbm] * 5,
         in_hbm,
     )(*(far_core(x) for x in (k, v, ak, av, decay.T)))
-    a = near_core(exchanged(first))
+    a = exchanged(first)
+    kv = a[:, 8 * TOK : 10 * TOK, :]
+    kv1 = near_core(shifted(kv, 1))
+    a = near_core(a)
     earlier = shifted(window, 2)
     second = call(
         pack_body, pltpu.HBM((PEERS, ROWS_B, HEAD), BF16),
@@ -329,16 +328,15 @@
         scratch_shapes=[pltpu.SemaphoreType.DMA],
     )(near_core(earlier), far_core(second))
     b = near_core(exchanged(second))
-    own, all_own, cols, rows = call(
+    own, cols, rows = call(
         state,
         (
             fast(BF16, STATE_ROWS, HEAD),
-            fast(BF16, STATE_ROWS + 2 * BLOCK, HEAD),
             fast(F32, BLOCK, HEAD),
             fast(F32, 16, BLOCK),
         ),
     )(a, lens)
-    near, far = near_core(shifted(all_own, 1)), near_core(shifted(own, 2))
+    far, near = near_core(shifted(own, 2)), near_core(shifted(own, 1))
     cols, rows = near_core(cols), near_core(rows)
     mixed, highest, inside, queries = call(
         within,
@@ -359,6 +357,7 @@
         finish,
         (shape(BLOCK, HEADS * HEAD), shape(BLOCK, HEADS * HEAD)),
         [
+            pltpu.VMEM((BLOCK, HEAD), BF16),
             pltpu.VMEM((BLOCK, 2 * HEAD), BF16),
             pltpu.VMEM((BLOCK, HEADS * HEAD), BF16),
             pltpu.VMEM((BLOCK, HEADS * HEAD), BF16),
@@ -367,6 +366,7 @@
         output=in_hbm,
     )(
         b,
+        kv1,
         near,
         far,
         cols,

time: 62.7 us -> 62.4 us (level)
  the two profiles are of different devices: /device:TPU:58 before, /device:TPU:56 now
where the time goes in v5:
time: 62.4 us; the launch traced here: 62.1 us
  waiting for transfers between devices  25.6 us (41%)
  starting transfers between devices  21.8 us (35%)
  Pallas kernels  13.1 us (21%)
  between operations  0.78 us (1%)
  local copies, waits for them, and re-layouts  0.74 us (1%)
    ppermute x4, waiting for transfers between devices, shifted(): lax.ppermute(block, 'ctx', [(i, i + distance) for i in range(count - dist...  17.3 us
    ppermute x4, starting transfers between devices, shifted(): lax.ppermute(block, 'ctx', [(i, i + distance) for i in range(count - dist...  12.9 us
    all_to_all x2, starting transfers between devices, exchanged(): lax.all_to_all(packed, 'uly', split_axis=0, concat_axis=0, tiled=True)  8.9 us
    all_to_all x2, waiting for transfers between devices, exchanged(): lax.all_to_all(packed, 'uly', split_axis=0, concat_axis=0, tiled=True)  8.26 us
    pallas_call x1, Pallas kernels, shards(): call(within, (fast(F32, BLOCK, 2 * HEADS * HEAD), fast(F32, BLOCK, HEADS...  3.77 us
    pallas_call x1, Pallas kernels, shards(): call(finish, (shape(BLOCK, HEADS * HEAD), shape(BLOCK, HEADS * HEAD)), [p...  3.1 us
    pallas_call x1, Pallas kernels, shards(): call(pack_first, (shape(PEERS, ROWS_A, HEAD), shape(PEERS, 2 * TOK, HEAD)...  2.35 us
    pallas_call x1, Pallas kernels, shards(): call(state, (fast(BF16, STATE_ROWS, HEAD), fast(F32, BLOCK, HEAD), fast(F...  1.98 us
  transfers between devices with their start and end apart: 6, of which 2 were waited for; matrix products, arithmetic and copies ran while one was open for 1% of the time, Pallas kernels for 12%

profile of v5, /device:TPU:56, one launch (start us, length us, event | category | flops | bytes accessed | tf_op | source)
XLA Modules:
  0.0 62.1 jit_solution(7582506175688802047)
XLA Ops:
  0.6 2.3 %shard_map.104 = (bf16[8,656,128]{2,1,0:T(8,128)(2,1)}, bf16[8,128,128]{2,1,0:T(8,128)(2,1)S(1)}) custom-call(bf16[64,4096]{1,0:T(8,128)(2,1)} %k.1, bf16[64,4096]{1,0:T(8,128)(2,1)} %v.1, bf16[64,1024]{1,0:T(8,128)(2,1)} %ak.1, bf16[64,1024]{1,0:T(8,128)(2,1)} %av.1, bf16[32,64]{1,0:T(8,128)(2,1)} %bitcast.5), custom_call_target="tpu_custom_call" | custom-call | tf_op jit(solution)/shard_map/pallas_call | solution.py:296
  3.0 0.0 copy-start
  3.0 0.0 copy-start.1
  3.0 4.4 %all-to-all-start.1 = ((bf16[8,656,128]{2,1,0:T(8,128)(2,1)}), bf16[8,656,128]{2,1,0:T(8,128)(2,1)S(1)}, u32[]{:S(2)}, u32[]{:S(2)}) async-start(bf16[8,656,128]{2,1,0:T(8,128)(2,1)} %get-tuple-element.12), calls=%async_computation.1 | async-start | bytes 2686976 | tf_op jit(solution)/shard_map/all_to_all | solution.py:286
  7.5 5.2 %collective-permute-start = (bf16[8,128,128]{2,1,0:T(8,128)(2,1)S(1)}, bf16[8,128,128]{2,1,0:T(8,128)(2,1)S(1)}, u32[]{:S(2)}, u32[]{:S(2)}) collective-permute-start(bf16[8,128,128]{2,1,0:T(8,128)(2,1)S(1)} %get-tuple-element.11), channel_id=1, source_target_pairs={{0,16},{8,24},{16,32},{24,40},{32,48},{40,56},{48,64},{56,72},{64,... | collective-permute-start | bytes 786440 | tf_op jit(solution)/shard_map/ppermute | solution.py:282
  12.6 0.0 copy-done
  12.6 1.2 %shard_map.105.packed = bf16[8,640,128]{2,1,0:T(8,128)(2,1)} custom-call(bf16[64,4096]{1,0:T(8,128)(2,1)S(1)} %copy-done, bf16[64,4096]{1,0:T(8,128)(2,1)S(1)} %copy-done.1), custom_call_target="tpu_custom_call" | custom-call | tf_op jit(solution)/shard_map/pallas_call | solution.py:318
  13.8 17.3 %collective-permute-done.earlier = bf16[8,128,128]{2,1,0:T(8,128)(2,1)S(1)} collective-permute-done((bf16[8,128,128]{2,1,0:T(8,128)(2,1)S(1)}, bf16[8,128,128]{2,1,0:T(8,128)(2,1)S(1)}, u32[]{:S(2)}, u32[]{:S(2)}) %collective-permute-start) | collective-permute-done | bytes 262176 | tf_op jit(solution)/shard_map/ppermute | solution.py:282
  31.2 0.8 %shard_map.106 = bf16[8,640,128]{2,1,0:T(8,128)(2,1)} custom-call(bf16[8,128,128]{2,1,0:T(8,128)(2,1)S(1)} %collective-permute-done.earlier, bf16[8,640,128]{2,1,0:T(8,128)(2,1)} %shard_map.105.packed), custom_call_target="tpu_custom_call", output_to_operand_aliasing={{}: (1, {})} | custom-call | tf_op jit(solution)/shard_map/pallas_call | solution.py:322
  31.9 0.0 copy-start.3
  31.9 0.0 all-to-all-done.1.a
  31.9 4.5 %all-to-all-start = ((bf16[8,640,128]{2,1,0:T(8,128)(2,1)}), bf16[8,640,128]{2,1,0:T(8,128)(2,1)S(1)}, u32[]{:S(2)}, u32[]{:S(2)}) async-start(bf16[8,640,128]{2,1,0:T(8,128)(2,1)} %shard_map.106), calls=%async_computation | async-start | bytes 2621440 | tf_op jit(solution)/shard_map/all_to_all | solution.py:286
  36.4 0.7 %slice.4 = bf16[8,128,128]{2,1,0:T(8,128)(2,1)} slice(bf16[8,656,128]{2,1,0:T(8,128)(2,1)S(1)} %all-to-all-done.1.a), slice={[0:8], [512:640], [0:128]} | slice | bytes 524288 | tf_op jit(solution)/shard_map/slice | solution.py:314
  37.1 1.9 %collective-permute-start.1 = (bf16[8,128,128]{2,1,0:T(8,128)(2,1)}, bf16[8,128,128]{2,1,0:T(8,128)(2,1)S(1)}, u32[]{:S(2)}, u32[]{:S(2)}) collective-permute-start(bf16[8,128,128]{2,1,0:T(8,128)(2,1)} %slice.4), channel_id=1, source_target_pairs={{0,8},{8,16},{16,24},{24,32},{32,40},{40,48},{48,56},{56,64},{64,7... | collective-permute-start | bytes 786440 | tf_op jit(solution)/shard_map/ppermute | solution.py:282
  39.0 0.0 copy-done.3
  39.0 2.0 %shard_map.107 = (bf16[528,128]{1,0:T(8,128)(2,1)}, f32[512,128]{1,0:T(8,128)S(1)}, f32[16,512]{1,0:T(8,128)S(1)}) custom-call(bf16[8,656,128]{2,1,0:T(8,128)(2,1)S(1)} %all-to-all-done.1.a, s32[1,64]{1,0:T(1,128)S(1)} %bitcast.4), custom_call_target="tpu_custom_call" | custom-call | tf_op jit(solution)/shard_map/pallas_call | solution.py:331
  41.0 1.9 %collective-permute-start.2 = (bf16[528,128]{1,0:T(8,128)(2,1)}, bf16[528,128]{1,0:T(8,128)(2,1)S(1)}, u32[]{:S(2)}, u32[]{:S(2)}) collective-permute-start(bf16[528,128]{1,0:T(8,128)(2,1)} %get-tuple-element.13), channel_id=1, source_target_pairs={{0,8},{8,16},{16,24},{24,32},{32,40},{40,48},{48,56},{56,64},{64,7... | collective-permute-start | bytes 405512 | tf_op jit(solution)/shard_map/ppermute | solution.py:282
  42.9 4.0 %collective-permute-start.3 = (bf16[528,128]{1,0:T(8,128)(2,1)}, bf16[528,128]{1,0:T(8,128)(2,1)S(1)}, u32[]{:S(2)}, u32[]{:S(2)}) collective-permute-start(bf16[528,128]{1,0:T(8,128)(2,1)} %get-tuple-element.13), channel_id=1, source_target_pairs={{0,16},{8,24},{16,32},{24,40},{32,48},{40,56},{48,64},{56,72},{64,... | collective-permute-start | bytes 405512 | tf_op jit(solution)/shard_map/ppermute | solution.py:282
  46.9 8.3 %all-to-all-done.b = bf16[8,640,128]{2,1,0:T(8,128)(2,1)S(1)} async-done(((bf16[8,640,128]{2,1,0:T(8,128)(2,1)}), bf16[8,640,128]{2,1,0:T(8,128)(2,1)S(1)}, u32[]{:S(2)}, u32[]{:S(2)}) %all-to-all-start) | async-done | bytes 1310752 | tf_op jit(solution)/shard_map/all_to_all | solution.py:286
  55.2 3.8 %shard_map.108 = (f32[512,1024]{1,0:T(8,128)S(1)}, f32[512,512]{1,0:T(8,128)S(1)}, f32[512,512]{1,0:T(8,128)S(1)}, bf16[2048,128]{1,0:T(8,128)(2,1)S(1)}) custom-call(bf16[8,656,128]{2,1,0:T(8,128)(2,1)S(1)} %all-to-all-done.1.a, bf16[8,640,128]{2,1,0:T(8,128)(2,1)S(1)} %all-to-all-done.b, f32[512,128]{1,0:T(8,128)S(1)} %get-tuple-element.14.cols, ...), custom_call_target="tpu_custom_call" | custom-call | tf_op jit(solution)/shard_map/pallas_call | solution.py:341
  58.9 0.0 collective-permute-done.2.near
  59.0 0.0 collective-permute-done.3.far
  59.0 0.0 collective-permute-done.1.kv1
  59.0 3.1 %shard_map.109 = (bf16[512,512]{1,0:T(8,128)(2,1)}, bf16[512,512]{1,0:T(8,128)(2,1)}) custom-call(bf16[8,640,128]{2,1,0:T(8,128)(2,1)S(1)} %all-to-all-done.b, bf16[8,128,128]{2,1,0:T(8,128)(2,1)S(1)} %collective-permute-done.1.kv1, bf16[528,128]{1,0:T(8,128)(2,1)S(1)} %collective-permute-done.2.near, bf16[528,128]{1,0:T(8,128)(2,1)S(1)} %collective-permute-done.3.far, ...), custom_call_target="tpu_custom_call" | custom-call | tf_op jit(solution)/shard_map/pallas_call | solution.py:356
  (3 shorter events, 0.0 us)
Async XLA Ops:
  3.0 9.6 %copy-start = (bf16[64,4096]{1,0:T(8,128)(2,1)S(1)}, bf16[64,4096]{1,0:T(8,128)(2,1)}, u32[]{:S(2)}) copy-start(bf16[64,4096]{1,0:T(8,128)(2,1)} %q.1) | copy-start | bytes 1572868
  3.0 9.6 %copy-start.1 = (bf16[64,4096]{1,0:T(8,128)(2,1)S(1)}, bf16[64,4096]{1,0:T(8,128)(2,1)}, u32[]{:S(2)}) copy-start(bf16[64,4096]{1,0:T(8,128)(2,1)} %aq.1) | copy-start | bytes 1572868
  3.0 28.9 %all-to-all-start.1 = ((bf16[8,656,128]{2,1,0:T(8,128)(2,1)}), bf16[8,656,128]{2,1,0:T(8,128)(2,1)S(1)}, u32[]{:S(2)}, u32[]{:S(2)}) async-start(bf16[8,656,128]{2,1,0:T(8,128)(2,1)} %get-tuple-element.12), calls=%async_computation.1 | async-start | bytes 2686976 | tf_op jit(solution)/shard_map/all_to_all | solution.py:286
  7.5 23.7 %collective-permute-start = (bf16[8,128,128]{2,1,0:T(8,128)(2,1)S(1)}, bf16[8,128,128]{2,1,0:T(8,128)(2,1)S(1)}, u32[]{:S(2)}, u32[]{:S(2)}) collective-permute-start(bf16[8,128,128]{2,1,0:T(8,128)(2,1)S(1)} %get-tuple-element.11), channel_id=1, source_target_pairs={{0,16},{8,24},{16,32},{24,40},{32,48},{40,56},{48,64},{56,72},{64,... | collective-permute-start | bytes 786440 | tf_op jit(solution)/shard_map/ppermute | solution.py:282
  31.9 7.1 %copy-start.3 = (s32[64]{0:T(128)S(1)}, s32[64]{0:T(128)}, u32[]{:S(2)}) copy-start(s32[64]{0:T(128)} %param.14) | copy-start | bytes 772
  31.9 23.2 %all-to-all-start = ((bf16[8,640,128]{2,1,0:T(8,128)(2,1)}), bf16[8,640,128]{2,1,0:T(8,128)(2,1)S(1)}, u32[]{:S(2)}, u32[]{:S(2)}) async-start(bf16[8,640,128]{2,1,0:T(8,128)(2,1)} %shard_map.106), calls=%async_computation | async-start | bytes 2621440 | tf_op jit(solution)/shard_map/all_to_all | solution.py:286
  37.1 21.9 %collective-permute-start.1 = (bf16[8,128,128]{2,1,0:T(8,128)(2,1)}, bf16[8,128,128]{2,1,0:T(8,128)(2,1)S(1)}, u32[]{:S(2)}, u32[]{:S(2)}) collective-permute-start(bf16[8,128,128]{2,1,0:T(8,128)(2,1)} %slice.4), channel_id=1, source_target_pairs={{0,8},{8,16},{16,24},{24,32},{32,40},{40,48},{48,56},{56,64},{64,7... | collective-permute-start | bytes 786440 | tf_op jit(solution)/shard_map/ppermute | solution.py:282
  41.0 17.9 %collective-permute-start.2 = (bf16[528,128]{1,0:T(8,128)(2,1)}, bf16[528,128]{1,0:T(8,128)(2,1)S(1)}, u32[]{:S(2)}, u32[]{:S(2)}) collective-permute-start(bf16[528,128]{1,0:T(8,128)(2,1)} %get-tuple-element.13), channel_id=1, source_target_pairs={{0,8},{8,16},{16,24},{24,32},{32,40},{40,48},{48,56},{56,64},{64,7... | collective-permute-start | bytes 405512 | tf_op jit(solution)/shard_map/ppermute | solution.py:282
  42.9 16.0 %collective-permute-start.3 = (bf16[528,128]{1,0:T(8,128)(2,1)}, bf16[528,128]{1,0:T(8,128)(2,1)S(1)}, u32[]{:S(2)}, u32[]{:S(2)}) collective-permute-start(bf16[528,128]{1,0:T(8,128)(2,1)} %get-tuple-element.13), channel_id=1, source_target_pairs={{0,16},{8,24},{16,32},{24,40},{32,48},{40,56},{48,64},{56,72},{64,... | collective-permute-start | bytes 405512 | tf_op jit(solution)/shard_map/ppermute | solution.py:282
  55.2 3.8 %copy-start.2 = (f32[512]{0:T(512)S(1)}, f32[512]{0:T(512)}, u32[]{:S(2)}) copy-start(f32[512]{0:T(512)} %param.13) | copy-start | bytes 6148
